TPU v7x, 256 devices: a whole 4x4x8 slice. The times are simulated.
256 devices in a mesh: ctx: 32 (over x, y, core), tp: 8 (over z).
Axes of the slice: x: 4, y: 4, z: 8, core: 2. Of those that a mesh axis runs over, the one named last changes fastest.
Arguments:
- hidden: bfloat16 [256, 8192], P(None, 'ctx'), may hold values from -6 to 6
- w_query: bfloat16 [8192, 8192], P('ctx', 'tp'), may hold values from -0.0625 to 0.0625
- w_key: bfloat16 [8192, 1024], P('ctx', 'tp'), may hold values from -0.375 to 0.375
- w_value: bfloat16 [8192, 1024], P('ctx', 'tp'), may hold values from -0.0625 to 0.0625
- w_out: bfloat16 [8192, 8192], P('tp', 'ctx'), may hold values from -0.1875 to 0.1875
- key_cache: bfloat16 [131072, 1024], P('ctx', 'tp'), may hold values from -130 to 130
- value_cache: bfloat16 [131072, 1024], P('ctx', 'tp'), may hold values from -6 to 6
- block_count: int32 [32], P('ctx'), may hold values from 512 to 4096, as said below
- positions: int32 [256], replicated, may hold values from 131072 to 131327, as said below
Outputs:
- attended: bfloat16 [256, 8192], P('tp', 'ctx')
Inputs may be any that keep to these rules, and one draw needn't show every extreme that they name: `block_count`: at least 512 slots of every block are valid; one block is full in every draw. The query positions are 131072 to 131327, each once, in any order.
All inputs are finite; a program needn't handle non-finite values.
Results may differ from a plain program's by a relative error of at most 0.02.
The roundings to bfloat16 on the way count: a program that leaves them out, or rounds other values in their place, can miss the bound.
Values may be sent and summed in bfloat16 or wider, within the bound.
No kernel may reach another device: no remote copies, remote signals or barrier semaphores. Data moves between devices by JAX's collectives and lax.ppermute only.
A program may use at most 128 MiB of HBM per device.

v0:
```python
import jax
import jax.numpy as jnp
from jax import lax
from jax.sharding import PartitionSpec as P

H = 64
KVH = 8
HD = 128


def combine_parts(first, second):
    largest = jnp.maximum(first[0], second[0])
    scale_one = jnp.exp(first[0] - largest)
    scale_two = jnp.exp(second[0] - largest)
    total = first[1] * scale_one + second[1] * scale_two
    summed = first[2] * scale_one[..., None] + second[2] * scale_two[..., None]
    return (largest, total, summed)


def own_part(query_rows, row_positions, new_keys, new_values, positions):
    own_scores = jnp.einsum(
        "qkgd,jkd->kgqj", query_rows, new_keys, preferred_element_type=jnp.float32
    )
    visible = (positions[None, :] <= row_positions[:, None])[None, None]
    own_top = jnp.max(jnp.where(visible, own_scores, -jnp.inf), axis=-1)
    own_weights = jnp.where(visible, jnp.exp(own_scores - own_top[..., None]), 0.0)
    own_total = jnp.sum(own_weights, axis=-1)
    own_sum = jnp.einsum(
        "kgqj,jkd->kgqd",
        own_weights.astype(jnp.bfloat16),
        new_values,
        preferred_element_type=jnp.float32,
    )
    return (own_top, own_total, own_sum)


def finish_rows(state, rows):
    largest, total, summed = state
    context = (summed / total[..., None]).transpose(2, 0, 1, 3)
    return context.reshape(rows, context.shape[1] * context.shape[2] * context.shape[3]).astype(
        jnp.bfloat16
    )


def on_device(
    hidden, w_query, w_key, w_value, w_out, key_cache, value_cache, block_count, positions
):
    group = H // KVH
    query_count = hidden.shape[0]
    local_heads = key_cache.shape[1] // HD
    query_full = jnp.dot(hidden, w_query, preferred_element_type=jnp.float32)
    key_full = jnp.dot(hidden, w_key, preferred_element_type=jnp.float32)
    value_full = jnp.dot(hidden, w_value, preferred_element_type=jnp.float32)
    query_full, key_full, value_full = lax.psum((query_full, key_full, value_full), "ctx")
    query_flat = (query_full * HD ** (-0.5)).astype(jnp.bfloat16)
    key_flat = key_full.astype(jnp.bfloat16)
    value_flat = value_full.astype(jnp.bfloat16)
    queries = query_flat.reshape(query_count, local_heads, group, HD)
    new_keys = key_flat.reshape(query_count, local_heads, HD)
    new_values = value_flat.reshape(query_count, local_heads, HD)
    block_rows = key_cache.shape[0]
    span = min(1024, block_rows)
    valid_count = block_count[0]

    def read_block(step, carry):
        largest, total, summed = carry
        start = step * span
        keys = lax.dynamic_slice_in_dim(key_cache, start, span, 0).reshape(span, local_heads, HD)
        values = lax.dynamic_slice_in_dim(value_cache, start, span, 0).reshape(
            span, local_heads, HD
        )
        scores = jnp.einsum("qkgd,tkd->kgqt", queries, keys, preferred_element_type=jnp.float32)
        valid = (start + jnp.arange(span, dtype=jnp.int32))[None, None, None, :] < valid_count
        block_top = jnp.max(jnp.where(valid, scores, -jnp.inf), axis=-1)
        updated = jnp.maximum(largest, block_top)
        weights = jnp.where(valid, jnp.exp(scores - updated[..., None]), 0.0)
        keep = jnp.exp(largest - updated)
        total = total * keep + jnp.sum(weights, axis=-1)
        summed = summed * keep[..., None] + jnp.einsum(
            "kgqt,tkd->kgqd",
            weights.astype(jnp.bfloat16),
            values,
            preferred_element_type=jnp.float32,
        )
        return (updated, total, summed)

    start_state = (
        jnp.full((local_heads, group, query_count), -jnp.inf, jnp.float32),
        jnp.zeros((local_heads, group, query_count), jnp.float32),
        jnp.zeros((local_heads, group, query_count, HD), jnp.float32),
    )
    largest, total, summed = lax.fori_loop(0, block_rows // span, read_block, start_state)
    overall = lax.pmax(largest, "ctx")
    factor = jnp.exp(largest - overall)
    total, summed = (
        lax.psum((total * factor).astype(jnp.bfloat16), "ctx").astype(jnp.float32),
        lax.psum((summed * factor[..., None]).astype(jnp.bfloat16), "ctx").astype(jnp.float32),
    )
    own = own_part(queries, positions, new_keys, new_values, positions)
    context = finish_rows(combine_parts((overall, total, summed), own), query_count)
    return lax.psum_scatter(
        jnp.dot(context, w_out, preferred_element_type=jnp.float32).astype(jnp.bfloat16),
        "tp",
        scatter_dimension=0,
        tiled=True,
    )


def solution(mesh):
    return jax.shard_map(
        on_device,
        mesh=mesh,
        in_specs=(
            P(None, "ctx"),
            P("ctx", "tp"),
            P("ctx", "tp"),
            P("ctx", "tp"),
            P("tp", "ctx"),
            P("ctx", "tp"),
            P("ctx", "tp"),
            P("ctx"),
            P(),
        ),
        out_specs=P("tp", "ctx"),
        check_vma=False,
    )
```

profile of v0, /device:TPU:1, one launch (start us, length us, event | category | flops | bytes accessed | tf_op | source)
XLA Modules:
  0.0 392.4 jit_solution(4337935916794274075)
XLA Ops:
  6.6 1.0 copy-done
  7.6 2.2 fusion.58
  10.1 0.2 fusion.60
  10.3 126.0 %all-reduce.8 = (bf16[256,128]{1,0:T(8,128)(2,1)S(1)}, bf16[256,128]{0,1:T(8,128)(2,1)S(1)}) all-reduce(f32[256,128]{1,0:T(8,128)S(1)} %fusion.59, f32[256,128]{0,1:T(8,128)S(1)} %fusion.60), channel_id=1, replica_groups=mesh['ctx'=32,'tp'=8] {'ctx'}, use_global_device_ids=true, to_apply=%region_7.8 | all-reduce | flops 65536 | bytes 393216 | tf_op jit(solution)/shard_map/psum | solution.py:54
  136.5 1.5 fusion.45
  138.2 32.6 %while.18 = (s32[]{:T(128)}, f32[1,8,256]{2,1,0:T(8,128)S(1)}, f32[1,8,256]{2,1,0:T(8,128)S(1)}, f32[1,8,256,128]{3,2,1,0:T(8,128)S(1)}, s32[]{:T(128)}, /*index...) while((s32[]{:T(128)}, f32[1,8,256]{2,1,0:T(8,128)S(1)}, ...), condition=%wide.region_4.0_spmd.clone, body=%wide.region_1.4_spmd.clone.sunk | while | flops 1091319808 | bytes 28446916 | solution.py:92
  138.2 0.7 add_compare_fusion.2
  138.9 2.2 fusion.77
  141.1 1.9 fusion.79
  143.0 3.3 fusion.80
  146.3 0.7 add_compare_fusion.2
  147.0 2.2 fusion.77
  149.2 1.9 fusion.79
  151.1 3.3 fusion.80
  154.5 0.7 add_compare_fusion.2
  155.1 2.2 fusion.77
  157.4 1.9 fusion.79
  159.3 3.3 fusion.80
  162.6 0.7 add_compare_fusion.2
  163.3 2.2 fusion.77
  165.6 1.9 fusion.79
  167.5 3.3 fusion.80
  170.8 0.3 copy.12
  171.1 68.7 %pmax.7 = f32[1,8,256]{2,1,0:T(8,128)S(1)} all-reduce(f32[1,8,256]{2,1,0:T(8,128)S(1)} %get-tuple-element.147), channel_id=1, replica_groups=mesh['ctx'=32,'tp'=8] {'ctx'}, use_global_device_ids=true, to_apply=%region_5.0 | all-reduce | flops 2048 | bytes 16384 | tf_op jit(solution)/shard_map/pmax | solution.py:93
  239.8 0.9 multiply_convert_fusion
  240.8 0.4 fusion.27
  241.2 0.4 fusion.30
  241.6 62.8 %psum.39 = bf16[1,8,256]{2,1,0:T(8,128)(2,1)S(1)} all-reduce(bf16[1,8,256]{2,1,0:T(8,128)(2,1)S(1)} %get-tuple-element.211), channel_id=1, replica_groups=mesh['ctx'=32,'tp'=8] {'ctx'}, use_global_device_ids=true, to_apply=%region_10.11 | all-reduce | flops 2048 | bytes 8192 | tf_op jit(solution)/shard_map/psum | solution.py:96
  304.5 47.9 %all-reduce.7.cloned.1.call-done = bf16[1,8,256,128]{2,3,1,0:T(8,128)(2,1)} async-done(((bf16[1,8,256,128]{2,3,1,0:T(8,128)(2,1)}), bf16[1,8,256,128]{2,3,1,0:T(8,128)(2,1)}) %all-reduce.7.cloned.1.call-update) | async-done | bytes 524304 | tf_op jit(solution)/shard_map/psum | solution.py:97
  352.3 1.7 fusion.35
  354.0 1.0 convolution_convert_fusion
  355.0 30.8 %reduce-scatter.2.cloned.1.call-done = bf16[32,256]{1,0:T(8,128)(2,1)} async-done(((bf16[256,256]{1,0:T(8,128)(2,1)}), bf16[32,256]{1,0:T(8,128)(2,1)}) %reduce-scatter.2.cloned.1.call-update) | async-done | bytes 16400 | tf_op jit(solution)/shard_map/reduce_scatter | solution.py:101
  (39 shorter events, 0.8 us)
Async XLA Ops:
  6.5 1.0 copy-start
  6.5 3.4 copy-start.1
  6.5 3.4 copy-start.2
  6.5 3.6 copy-start.3
  6.5 129.8 %copy-start.4 = (s32[256]{0:T(256)S(1)}, s32[256]{0:T(256)}, u32[]{:S(2)}) copy-start(s32[256]{0:T(256)} %param.19) | copy-start | bytes 3076
  6.5 129.9 %all-reduce.5.cloned.1.call-start = ((), (), s32[]{:S(2)}) async-start(), calls=%async_computation.1 | async-start | bytes 2097152 | tf_op jit(solution)/shard_map/psum | solution.py:54
  9.8 342.5 %all-reduce.7.cloned.1.call-start = ((), (), s32[]{:S(2)}) async-start(), calls=%async_computation.2 | async-start | bytes 1048576 | tf_op jit(solution)/shard_map/psum | solution.py:97
  240.7 145.1 %reduce-scatter.2.cloned.1.call-start = ((), (), s32[]{:S(2)}) async-start(), calls=%async_computation.3 | async-start | bytes 147456 | tf_op jit(solution)/shard_map/reduce_scatter | solution.py:101
  352.3 1.7 copy-start.5
Sparse Core Ops, SparseCore 0:
  10.6 118.8 all-reduce.4
  240.9 111.4 all-reduce.6
  355.1 30.6 reduce-scatter.1
where the time goes:
time: 397 us; the launch traced here: 392 us
  blocking collectives  257 us (65%)
  waiting for transfers between devices  78.8 us (20%)
  matrix products  27.7 us (7%)
  between operations  13.3 us (3%)
  other arithmetic  13.2 us (3%)
    psum x1, blocking collectives, on_device(): lax.psum((query_full, key_full, value_full), 'ctx')  126 us
    pmax x1, blocking collectives, on_device(): overall = lax.pmax(largest, 'ctx')  68.7 us
    psum x1, blocking collectives, on_device(): lax.psum((total * factor).astype(jnp.bfloat16), 'ctx').astype(jnp.float32)  62.8 us
    psum x1, waiting for transfers between devices, on_device(): lax.psum((summed * factor[..., None]).astype(jnp.bfloat16), 'ctx')  47.9 us
    reduce_scatter x1, waiting for transfers between devices, on_device(): lax.psum_scatter(jnp.dot(context, w_out, preferred_element_type=jnp.float...  30.8 us
    dot_general x4, matrix products, read_block(): jnp.einsum('kgqt,tkd->kgqd', weights.astype(jnp.bfloat16), values, prefer...  13.1 us
    dot_general x4, matrix products, read_block(): jnp.einsum('qkgd,tkd->kgqt', queries, keys, preferred_element_type=jnp.fl...  8.89 us
  transfers between devices with their start and end apart: 3, of which 2 were waited for; matrix products, arithmetic and copies ran while one was open for 0% of the time, Pallas kernels for 0%

commit v1 on v0

v1 whole, which is shorter than its diff:
```python
import functools

import jax
import jax.numpy as jnp
from jax import lax
from jax.experimental import pallas as pl
from jax.experimental.pallas import tpu as pltpu
from jax.sharding import PartitionSpec as P

H = 64
KVH = 8
HD = 128
SPAN = 2048
STEP = 512
LOG2E = 1.4426950408889634
LARGE = 2.0**100
SMALL = 2.0**-60
ROWS_BY_ROWS = (((1,), (1,)), ((), ()))
VMEM = pl.BlockSpec(memory_space=pltpu.VMEM)
SMEM = pl.BlockSpec(memory_space=pltpu.SMEM)
KERNEL = pltpu.CompilerParams(vmem_limit_bytes=40 * 2**20)


def sum_kernel(width, pieces, queries, other):
    total = jnp.sum(pieces[...], axis=0)
    rows = (total[:, :width] * HD ** (-0.5)).astype(jnp.bfloat16)
    for place in range(queries.shape[0]):
        queries[place] = rows
    other[...] = total[:, width:].astype(jnp.bfloat16)


def three_parts(value):
    high = value.astype(jnp.bfloat16).astype(jnp.float32)
    rest = value - high
    middle = rest.astype(jnp.bfloat16).astype(jnp.float32)
    return (high, middle, rest - middle)


def attend_kernel(
    heads, count, queries, keys0, values0, keys1, values1, new_keys, new_values,
    row_positions, key_positions, out, wide, reference, total, summed,
):
    rows = queries.shape[0]
    blocks = ((keys0, values0), (keys1, values1))
    lane = lax.broadcasted_iota(jnp.int32, (rows, HD), 1)
    visible = key_positions[...] <= row_positions[...]

    def own_scores(head):
        scores = lax.dot_general(
            queries[:, head * HD : (head + 1) * HD], new_keys[...], ROWS_BY_ROWS,
            preferred_element_type=jnp.float32,
        )
        return jnp.where(visible, scores, -jnp.inf)

    for head in range(heads):
        at = slice(head * rows, (head + 1) * rows)
        query = queries[:, head * HD : (head + 1) * HD]
        sample = lax.dot_general(
            query, keys0[:256, :], ROWS_BY_ROWS, preferred_element_type=jnp.float32
        )
        scores = own_scores(head)
        top = jnp.maximum(
            jnp.max(sample, axis=1, keepdims=True), jnp.max(scores, axis=1, keepdims=True)
        )
        level = jnp.broadcast_to(top, (rows, HD)).astype(jnp.bfloat16).astype(jnp.float32)
        wide[at, :HD] = query
        wide[at, HD:] = jnp.where(lane == 0, -level, jnp.where(lane == 1, 1.0, 0.0)).astype(
            jnp.bfloat16
        )
        weights = jnp.exp2((scores - level) * LOG2E)
        reference[at] = level
        total[at] = jnp.broadcast_to(jnp.sum(weights, axis=1, keepdims=True), (rows, HD))
        summed[at] = jnp.dot(
            weights.astype(jnp.bfloat16), new_values[...], preferred_element_type=jnp.float32
        )

    span_lane = lax.broadcasted_iota(jnp.int32, (SPAN, HD), 1)
    span_row = lax.broadcasted_iota(jnp.int32, (SPAN, HD), 0)

    for which, (keys, values) in enumerate(blocks):
        limit = count[which]

        def read_span(step, carry, keys=keys, values=values, limit=limit):
            start = pl.multiple_of(step * SPAN, SPAN)
            bias = jnp.where(span_row + start < limit, 0.0, -1e30)
            extra = jnp.where(span_lane == 0, 1.0, jnp.where(span_lane == 1, bias, 0.0))
            key = jnp.concatenate(
                [keys[pl.ds(start, SPAN), :], extra.astype(jnp.bfloat16)], axis=1
            )
            value = values[pl.ds(start, SPAN), :]
            for head in range(heads):
                at = slice(head * rows, (head + 1) * rows)
                scores = lax.dot_general(
                    wide[at], key, ROWS_BY_ROWS, preferred_element_type=jnp.float32
                )
                weights = jnp.exp2(scores * LOG2E)
                total[at] = total[at] + jnp.sum(weights, axis=1, keepdims=True)
                summed[at] = summed[at] + jnp.dot(
                    weights.astype(jnp.bfloat16), value, preferred_element_type=jnp.float32
                )
            return carry

        lax.fori_loop(0, (limit + SPAN - 1) // SPAN, read_span, 0)

    in_range = jnp.logical_and(jnp.max(total[...]) < LARGE, jnp.min(total[...]) > SMALL)

    @pl.when(jnp.logical_not(in_range))
    def _():
        reference[...] = jnp.full_like(reference, -jnp.inf)
        total[...] = jnp.zeros_like(total)
        summed[...] = jnp.zeros_like(summed)

        def update(at, scores, value):
            before = reference[at]
            now = jnp.maximum(before, jnp.max(scores, axis=1, keepdims=True))
            keep = jnp.exp(before - now)
            weights = jnp.exp(scores - now[:, :1])
            total[at] = total[at] * keep + jnp.sum(weights, axis=1, keepdims=True)
            summed[at] = summed[at] * keep + jnp.dot(
                weights.astype(jnp.bfloat16), value, preferred_element_type=jnp.float32
            )
            reference[at] = now

        for which, (keys, values) in enumerate(blocks):
            limit = count[which]

            def read_step(step, carry, keys=keys, values=values, limit=limit):
                start = pl.multiple_of(step * STEP, STEP)
                valid = start + lax.broadcasted_iota(jnp.int32, (1, STEP), 1) < limit
                key = keys[pl.ds(start, STEP), :]
                value = values[pl.ds(start, STEP), :]
                for head in range(heads):
                    scores = lax.dot_general(
                        queries[:, head * HD : (head + 1) * HD], key, ROWS_BY_ROWS,
                        preferred_element_type=jnp.float32,
                    )
                    update(
                        slice(head * rows, (head + 1) * rows),
                        jnp.where(valid, scores, -jnp.inf),
                        value,
                    )
                return carry

            lax.fori_loop(0, (limit + STEP - 1) // STEP, read_step, 0)
        for head in range(heads):
            update(slice(head * rows, (head + 1) * rows), own_scores(head), new_values[...])

    statistics = jnp.zeros((rows, HD), jnp.float32)
    for head in range(heads):
        at = slice(head * rows, (head + 1) * rows)
        out[:, head * HD : (head + 1) * HD] = summed[at].astype(jnp.bfloat16)
        parts = three_parts(reference[at]) + three_parts(total[at])
        for place, part in enumerate(parts):
            statistics = jnp.where(lane == 8 * head + place, part, statistics)
    out[:, heads * HD :] = statistics.astype(jnp.bfloat16)


def combine_kernel(heads, pieces, out):
    sources, rows, _ = pieces.shape
    width = heads * HD
    statistics = pieces[:, :, width:].reshape(sources * rows, HD)
    place = lax.broadcasted_iota(jnp.int32, (HD, width), 0)
    column = lax.broadcasted_iota(jnp.int32, (HD, width), 1)
    own = place // 8 == column // HD
    pick_top = jnp.where(own & (place % 8 < 3), 1.0, 0.0).astype(jnp.bfloat16)
    pick_total = jnp.where(own & (place % 8 >= 3) & (place % 8 < 6), 1.0, 0.0)
    tops = jnp.dot(statistics, pick_top, preferred_element_type=jnp.float32)
    totals = jnp.dot(
        statistics, pick_total.astype(jnp.bfloat16), preferred_element_type=jnp.float32
    )
    tops = tops.reshape(sources, rows, width)
    totals = totals.reshape(sources, rows, width)
    scale = jnp.exp(tops - jnp.max(tops, axis=0, keepdims=True))
    summed = jnp.sum(scale * pieces[:, :, :width].astype(jnp.float32), axis=0)
    context = (summed / jnp.sum(scale * totals, axis=0)).astype(jnp.bfloat16)
    for target in range(out.shape[0]):
        out[target] = context


def on_device(
    shards, hidden, w_query, w_key, w_value, w_out, key_cache, value_cache, block_count, positions
):
    query_count = hidden.shape[0]
    chips = shards // 2
    rows = query_count // chips
    half = w_query.shape[1] // 2
    heads = half // HD
    place = lax.axis_index("ctx")
    chip = place // 2
    first = place % 2 == 0
    swap = [(index, index ^ 1) for index in range(shards)]
    same_core = [[2 * index + core for index in range(chips)] for core in range(2)]

    def exchange(array):
        return lax.all_to_all(array, "ctx", 0, 0, axis_index_groups=same_core)

    low, high = w_query[:, :half], w_query[:, half:]
    own_columns = jnp.concatenate(
        [jnp.where(first, low, high), jnp.where(first, w_key, w_value)], axis=1
    )
    sent_columns = jnp.concatenate(
        [jnp.where(first, high, low), jnp.where(first, w_value, w_key)], axis=1
    )
    hidden_other = lax.ppermute(hidden, "ctx", swap)
    columns_other = lax.ppermute(sent_columns, "ctx", swap)
    keys_other = lax.ppermute(key_cache, "ctx", swap)
    values_other = lax.ppermute(value_cache, "ctx", swap)
    count_other = lax.ppermute(block_count, "ctx", swap)
    partial = jnp.dot(hidden, own_columns, preferred_element_type=jnp.float32) + jnp.dot(
        hidden_other, columns_other, preferred_element_type=jnp.float32
    )
    pieces = exchange(partial.reshape(chips, rows, half + HD))
    query_rows, new_own = pl.pallas_call(
        functools.partial(sum_kernel, half),
        out_shape=(
            jax.ShapeDtypeStruct((chips, rows, half), jnp.bfloat16),
            jax.ShapeDtypeStruct((rows, HD), jnp.bfloat16),
        ),
        in_specs=[VMEM],
        out_specs=(VMEM, VMEM),
        compiler_params=KERNEL,
    )(pieces)
    new_other = lax.ppermute(new_own, "ctx", swap)
    queries = exchange(query_rows).reshape(query_count, half)
    padding = ((0, HD - rows), (0, 0))
    new_keys = jnp.pad(jnp.where(first, new_own, new_other), padding)
    new_values = jnp.pad(jnp.where(first, new_other, new_own), padding)
    key_positions = jnp.pad(
        lax.dynamic_slice_in_dim(positions, chip * rows, rows, 0),
        (0, HD - rows),
        constant_values=jnp.iinfo(jnp.int32).max,
    )[None, :]
    local = pl.pallas_call(
        functools.partial(attend_kernel, heads),
        out_shape=jax.ShapeDtypeStruct((query_count, half + HD), jnp.bfloat16),
        in_specs=[SMEM] + [VMEM] * 9,
        out_specs=VMEM,
        scratch_shapes=[
            pltpu.VMEM((heads * query_count, 2 * HD), jnp.bfloat16),
            pltpu.VMEM((heads * query_count, HD), jnp.float32),
            pltpu.VMEM((heads * query_count, HD), jnp.float32),
            pltpu.VMEM((heads * query_count, HD), jnp.float32),
        ],
        compiler_params=KERNEL,
    )(
        jnp.concatenate([block_count, count_other]),
        queries,
        key_cache,
        value_cache,
        keys_other,
        values_other,
        new_keys,
        new_values,
        positions[:, None],
        key_positions,
    )
    groups = exchange(local.reshape(chips, rows, half + HD))
    context_rows = pl.pallas_call(
        functools.partial(combine_kernel, heads),
        out_shape=jax.ShapeDtypeStruct((chips, rows, half), jnp.bfloat16),
        in_specs=[VMEM],
        out_specs=VMEM,
        compiler_params=KERNEL,
    )(groups)
    context = exchange(context_rows).reshape(query_count, half)
    context_other = lax.ppermute(context, "ctx", swap)
    start = (place % 2) * half
    out_own = lax.dynamic_slice_in_dim(w_out, start, half, 0)
    out_other = lax.dynamic_slice_in_dim(w_out, half - start, half, 0)
    attended = jnp.dot(context, out_own, preferred_element_type=jnp.float32) + jnp.dot(
        context_other, out_other, preferred_element_type=jnp.float32
    )
    parts = lax.axis_size("tp")
    attended = attended.astype(jnp.bfloat16).reshape(parts, query_count // parts, -1)
    received = lax.all_to_all(attended, "tp", 0, 0)
    return jnp.sum(received.astype(jnp.float32), axis=0).astype(jnp.bfloat16)


def solution(mesh):
    return jax.shard_map(
        functools.partial(on_device, mesh.shape["ctx"]),
        mesh=mesh,
        in_specs=(
            P(None, "ctx"),
            P("ctx", "tp"),
            P("ctx", "tp"),
            P("ctx", "tp"),
            P("tp", "ctx"),
            P("ctx", "tp"),
            P("ctx", "tp"),
            P("ctx"),
            P(),
        ),
        out_specs=P("tp", "ctx"),
        check_vma=False,
    )
```

time: 397 us -> 125 us (0.31)
  blocking collectives: 257 us -> 48.5 us
  waiting for transfers between devices: 78.8 us -> 18.1 us
  Pallas kernels: 0 us -> 29.5 us
  matrix products: 27.7 us -> 1.83 us
  starting transfers between devices: 0.12 us -> 20 us
  between operations: 13.3 us -> 0.84 us
  other arithmetic: 13.2 us -> 3.5 us
    psum x2 -> x0, blocking collectives: 189 us -> none  [the longest x1 126 us: on_device(): lax.psum((query_full, key_full, value_full), 'ctx')]
    pmax x1 -> x0, blocking collectives: 68.7 us -> none  [on_device(): overall = lax.pmax(largest, 'ctx')]
    all_to_all x0 -> x3, blocking collectives: none -> 48.5 us  [the longest x2 32.6 us: exchange(): return lax.all_to_all(array, 'ctx', 0, 0, axis_index_groups=same_core)]
    psum x2 -> x0, waiting for transfers between devices: 47.9 us -> none  [the longest x1 47.9 us: on_device(): lax.psum((summed * factor[..., None]).astype(jnp.bfloat16), 'ctx')]
    reduce_scatter x1 -> x0, waiting for transfers between devices: 30.8 us -> none  [on_device(): lax.psum_scatter(jnp.dot(context, w_out, preferred_element_type=jnp.float...]
    pallas_call x0 -> x3, Pallas kernels: none -> 29.5 us  [the longest x1 29.1 us: on_device(): pl.pallas_call(functools.partial(attend_kernel, heads), out_shape=jax.Sha...]
    dot_general x14 -> x4, matrix products: 27.7 us -> 1.83 us  [the longest x1 1.11 us: on_device(): jnp.dot(hidden_other, columns_other, preferred_element_type=jnp.float32)]
    all_to_all x0 -> x2, waiting for transfers between devices: none -> 16.9 us  [exchange(): return lax.all_to_all(array, 'ctx', 0, 0, axis_index_groups=same_core)]
  transfers between devices with their start and end apart: 3 -> 9, of which waited for: 2 -> 4; matrix products, arithmetic and copies ran while one was open for 0% -> 2% of each run, Pallas kernels for 0% -> 0%
where the time goes in v1:
time: 125 us; the launch traced here: 123 us
  blocking collectives  48.5 us (39%)
  Pallas kernels  29.5 us (24%)
  starting transfers between devices  20 us (16%)
  waiting for transfers between devices  18.1 us (14%)
  other arithmetic  3.5 us (3%)
  matrix products  1.83 us (1%)
    all_to_all x2, blocking collectives, exchange(): return lax.all_to_all(array, 'ctx', 0, 0, axis_index_groups=same_core)  32.6 us
    pallas_call x1, Pallas kernels, on_device(): pl.pallas_call(functools.partial(attend_kernel, heads), out_shape=jax.Sha...  29.1 us
    all_to_all x2, waiting for transfers between devices, exchange(): return lax.all_to_all(array, 'ctx', 0, 0, axis_index_groups=same_core)  16.9 us
    all_to_all x1, blocking collectives, on_device(): received = lax.all_to_all(attended, 'tp', 0, 0)  15.9 us
    all_to_all x2, starting transfers between devices, exchange(): return lax.all_to_all(array, 'ctx', 0, 0, axis_index_groups=same_core)  8.68 us
    ppermute x1, starting transfers between devices, on_device(): context_other = lax.ppermute(context, 'ctx', swap)  3.6 us
    ppermute x1, starting transfers between devices, on_device(): columns_other = lax.ppermute(sent_columns, 'ctx', swap)  3.33 us
  transfers between devices with their start and end apart: 9, of which 4 were waited for; matrix products, arithmetic and copies ran while one was open for 2% of the time, Pallas kernels for 0%

profile of v1, /device:TPU:1, one launch (start us, length us, event | category | flops | bytes accessed | tf_op | source)
XLA Modules:
  0.0 123.3 jit_solution(1480364490324586149)
XLA Ops:
  0.0 1.2 broadcast_select_fusion
  1.2 0.9 broadcast_select_fusion.2
  2.1 0.0 copy-start.4
  2.1 3.3 %collective-permute-start.1 = (bf16[256,640]{1,0:T(8,128)(2,1)S(1)}, bf16[256,640]{1,0:T(8,128)(2,1)S(1)}, u32[]{:S(2)}, u32[]{:S(2)}) collective-permute-start(bf16[256,640]{1,0:T(8,128)(2,1)S(1)} %pad_maximum_fusion), channel_id=1, source_target_pairs={{0,8},{8,0},{16,24},{24,16},{32,40},{40,32},{48,56},{56,48},{64,72... | collective-permute-start | bytes 983048 | tf_op jit(solution)/shard_map/ppermute | solution.py:205
  5.5 0.8 collective-permute-start.2
  6.2 0.0 collective-permute-start.3
  6.2 0.5 collective-permute-start.4
  6.7 0.3 fusion.1
  7.0 0.3 collective-permute-done.2
  7.3 0.0 collective-permute-done.1
  7.3 1.1 convolution_add_fusion
  8.5 5.2 %all-to-all-start = ((f32[16,16,640]{2,1,0:T(8,128)}), f32[16,16,640]{2,1,0:T(8,128)S(1)}, u32[]{:S(2)}, u32[]{:S(2)}) async-start(f32[16,16,640]{2,1,0:T(8,128)} %bitcast.1), calls=%async_computation | async-start | bytes 1310720 | tf_op jit(solution)/shard_map/all_to_all | solution.py:195
  13.6 0.0 copy-start.2
  13.6 0.7 collective-permute-start
  15.0 0.1 dynamic_slice.9
  15.1 0.1 copy.10.row_positions
  15.3 9.8 %all-to-all-done.pieces = f32[16,16,640]{2,1,0:T(8,128)S(1)} async-done(((f32[16,16,640]{2,1,0:T(8,128)}), f32[16,16,640]{2,1,0:T(8,128)S(1)}, u32[]{:S(2)}, u32[]{:S(2)}) %all-to-all-start) | async-done | bytes 655392 | tf_op jit(solution)/shard_map/all_to_all | solution.py:195
  25.1 0.7 copy-done.3
  25.8 2.4 %collective-permute-start.5 = (bf16[16,128]{1,0:T(8,128)(2,1)S(1)}, bf16[16,128]{1,0:T(8,128)(2,1)S(1)}, u32[]{:S(2)}, u32[]{:S(2)}) collective-permute-start(bf16[16,128]{1,0:T(8,128)(2,1)S(1)} %get-tuple-element.8), channel_id=1, source_target_pairs={{0,8},{8,0},{16,24},{24,16},{32,40},{40,32},{48,56},{56,48},{64,72... | collective-permute-start | bytes 12296 | tf_op jit(solution)/shard_map/ppermute | solution.py:223
  28.2 3.5 %all-to-all-start.1 = ((bf16[16,16,512]{2,1,0:T(8,128)(2,1)}), bf16[16,16,512]{2,1,0:T(8,128)(2,1)S(1)}, u32[]{:S(2)}, u32[]{:S(2)}) async-start(bf16[16,16,512]{2,1,0:T(8,128)(2,1)} %copy-done.3), calls=%async_computation.1 | async-start | bytes 524288 | tf_op jit(solution)/shard_map/all_to_all | solution.py:195
  31.8 0.8 pad_add_fusion.count
  32.6 7.1 %all-to-all-done.1 = bf16[16,16,512]{2,1,0:T(8,128)(2,1)S(1)} async-done(((bf16[16,16,512]{2,1,0:T(8,128)(2,1)}), bf16[16,16,512]{2,1,0:T(8,128)(2,1)S(1)}, u32[]{:S(2)}, u32[]{:S(2)}) %all-to-all-start.1) | async-done | bytes 262176 | tf_op jit(solution)/shard_map/all_to_all | solution.py:195
  39.7 29.1 %shard_map.92 = bf16[256,640]{1,0:T(8,128)(2,1)S(1)} custom-call(s32[2]{0:T(128)S(1)} %pad_add_fusion.count, bf16[256,512]{1,0:T(8,128)(2,1)S(1)} %bitcast.16, bf16[4096,128]{1,0:T(8,128)(2,1)S(1)} %copy-done.1, bf16[4096,128]{1,0:T(8,128)(2,1)S(1)} %copy-done.2, bf16[4096,128]{1,0:T(8,128)(2,1)} %collective-permute-done.3.keys1, ...), custom_call_target="tpu_custom_call" | custom-call | tf_op jit(solution)/shard_map/pallas_call | solution.py:233
  68.8 21.9 %all_to_all.25.pieces = bf16[16,16,640]{2,1,0:T(8,128)(2,1)S(1)} all-to-all(bf16[16,16,640]{2,1,0:T(8,128)(2,1)S(1)} %bitcast.15), channel_id=1, replica_groups={{0,16,32,48,64,80,96,112,128,144,160,176,192,208,224,240},{8,24,40,56,7..., dimensions={0} | all-to-all | bytes 655360 | tf_op jit(solution)/shard_map/all_to_all | solution.py:195
  90.7 0.4 shard_map.93
  91.0 10.7 %all_to_all.26 = bf16[16,16,512]{2,1,0:T(8,128)(2,1)S(1)} all-to-all(bf16[16,16,512]{2,1,0:T(8,128)(2,1)S(1)} %shard_map.93), channel_id=1, replica_groups={{0,16,32,48,64,80,96,112,128,144,160,176,192,208,224,240},{8,24,40,56,7..., dimensions={0} | all-to-all | bytes 524288 | tf_op jit(solution)/shard_map/all_to_all | solution.py:195
  101.8 3.6 %collective-permute-start.6 = (bf16[256,512]{1,0:T(8,128)(2,1)S(1)}, bf16[256,512]{1,0:T(8,128)(2,1)S(1)}, u32[]{:S(2)}, u32[]{:S(2)}) collective-permute-start(bf16[256,512]{1,0:T(8,128)(2,1)S(1)} %bitcast.17), channel_id=1, source_target_pairs={{0,8},{8,0},{16,24},{24,16},{32,40},{40,32},{48,56},{56,48},{64,72... | collective-permute-start | bytes 786440 | tf_op jit(solution)/shard_map/ppermute | solution.py:266
  105.4 0.2 fusion.6
  105.6 0.9 collective-permute-done.6
  106.5 0.2 fusion
  106.8 15.9 %all_to_all.27 = bf16[8,32,256]{2,1,0:T(8,128)(2,1)S(1)} all-to-all(bf16[8,32,256]{2,1,0:T(8,128)(2,1)S(1)} %bitcast.19), channel_id=1, replica_groups=mesh['ctx'=32,'tp'=8] {'tp'}, dimensions={0} | all-to-all | bytes 262144 | tf_op jit(solution)/shard_map/all_to_all | solution.py:275
  122.7 0.6 reduce_sum.12
  (19 shorter events, 0.1 us)
Async XLA Ops:
  0.0 105.4 %copy-start = (bf16[1024,256]{1,0:T(8,128)(2,1)S(1)}, bf16[1024,256]{1,0:T(8,128)(2,1)}, u32[]{:S(2)}) copy-start(bf16[1024,256]{1,0:T(8,128)(2,1)} %param.13) | copy-start | bytes 1572868
  0.0 6.2 %copy-start.1 = (bf16[4096,128]{1,0:T(8,128)(2,1)S(1)}, bf16[4096,128]{1,0:T(8,128)(2,1)}, u32[]{:S(2)}) copy-start(bf16[4096,128]{1,0:T(8,128)(2,1)} %keys0.1) | copy-start | bytes 3145732
  2.1 3.4 %copy-start.4 = (bf16[256,256]{1,0:T(8,128)(2,1)S(1)}, bf16[256,256]{1,0:T(8,128)(2,1)}, u32[]{:S(2)}) copy-start(bf16[256,256]{1,0:T(8,128)(2,1)} %param.9) | copy-start | bytes 393220
  2.1 5.2 %collective-permute-start.1 = (bf16[256,640]{1,0:T(8,128)(2,1)S(1)}, bf16[256,640]{1,0:T(8,128)(2,1)S(1)}, u32[]{:S(2)}, u32[]{:S(2)}) collective-permute-start(bf16[256,640]{1,0:T(8,128)(2,1)S(1)} %pad_maximum_fusion), channel_id=1, source_target_pairs={{0,8},{8,0},{16,24},{24,16},{32,40},{40,32},{48,56},{56,48},{64,72... | collective-permute-start | bytes 983048 | tf_op jit(solution)/shard_map/ppermute | solution.py:205
  5.5 1.9 %collective-permute-start.2 = (bf16[256,256]{1,0:T(8,128)(2,1)S(1)}, bf16[256,256]{1,0:T(8,128)(2,1)S(1)}, u32[]{:S(2)}, u32[]{:S(2)}) collective-permute-start(bf16[256,256]{1,0:T(8,128)(2,1)S(1)} %copy-done.4), channel_id=1, source_target_pairs={{0,8},{8,0},{16,24},{24,16},{32,40},{40,32},{48,56},{56,48},{64,72... | collective-permute-start | bytes 393224 | tf_op jit(solution)/shard_map/ppermute | solution.py:204
  6.2 26.3 %collective-permute-start.3 = (bf16[4096,128]{1,0:T(8,128)(2,1)S(1)}, bf16[4096,128]{1,0:T(8,128)(2,1)}, u32[]{:S(2)}, u32[]{:S(2)}) collective-permute-start(bf16[4096,128]{1,0:T(8,128)(2,1)S(1)} %copy-done.1), channel_id=1, source_target_pairs={{0,8},{8,0},{16,24},{24,16},{32,40},{40,32},{48,56},{56,48},{64,72... | collective-permute-start | bytes 3145736 | tf_op jit(solution)/shard_map/ppermute | solution.py:206
  6.2 26.3 %collective-permute-start.4 = (bf16[4096,128]{1,0:T(8,128)(2,1)}, bf16[4096,128]{1,0:T(8,128)(2,1)}, u32[]{:S(2)}, u32[]{:S(2)}) collective-permute-start(bf16[4096,128]{1,0:T(8,128)(2,1)} %values0.1), channel_id=1, source_target_pairs={{0,8},{8,0},{16,24},{24,16},{32,40},{40,32},{48,56},{56,48},{64,72... | collective-permute-start | bytes 3145736 | tf_op jit(solution)/shard_map/ppermute | solution.py:207
  8.4 6.6 %copy-start.5 = (s32[256]{0:T(256)S(1)}, s32[256]{0:T(256)}, u32[]{:S(2)}) copy-start(s32[256]{0:T(256)} %param.17) | copy-start | bytes 3076
  8.5 16.6 %all-to-all-start = ((f32[16,16,640]{2,1,0:T(8,128)}), f32[16,16,640]{2,1,0:T(8,128)S(1)}, u32[]{:S(2)}, u32[]{:S(2)}) async-start(f32[16,16,640]{2,1,0:T(8,128)} %bitcast.1), calls=%async_computation | async-start | bytes 1310720 | tf_op jit(solution)/shard_map/all_to_all | solution.py:195
  13.6 26.1 %copy-start.2 = (bf16[4096,128]{1,0:T(8,128)(2,1)S(1)}, bf16[4096,128]{1,0:T(8,128)(2,1)}, u32[]{:S(2)}) copy-start(bf16[4096,128]{1,0:T(8,128)(2,1)} %values0.1) | copy-start | bytes 3145732
  13.6 18.1 %collective-permute-start = (s32[1]{0:T(128)}, s32[1]{0:T(128)}, u32[]{:S(2)}, u32[]{:S(2)}) collective-permute-start(s32[1]{0:T(128)} %param.16), channel_id=1, source_target_pairs={{0,8},{8,0},{16,24},{24,16},{32,40},{40,32},{48,56},{56,48},{64,72... | collective-permute-start | bytes 20 | tf_op jit(solution)/shard_map/ppermute | solution.py:208
  25.1 0.7 copy-start.3
  25.8 6.7 %collective-permute-start.5 = (bf16[16,128]{1,0:T(8,128)(2,1)S(1)}, bf16[16,128]{1,0:T(8,128)(2,1)S(1)}, u32[]{:S(2)}, u32[]{:S(2)}) collective-permute-start(bf16[16,128]{1,0:T(8,128)(2,1)S(1)} %get-tuple-element.8), channel_id=1, source_target_pairs={{0,8},{8,0},{16,24},{24,16},{32,40},{40,32},{48,56},{56,48},{64,72... | collective-permute-start | bytes 12296 | tf_op jit(solution)/shard_map/ppermute | solution.py:223
  28.2 11.5 %all-to-all-start.1 = ((bf16[16,16,512]{2,1,0:T(8,128)(2,1)}), bf16[16,16,512]{2,1,0:T(8,128)(2,1)S(1)}, u32[]{:S(2)}, u32[]{:S(2)}) async-start(bf16[16,16,512]{2,1,0:T(8,128)(2,1)} %copy-done.3), calls=%async_computation.1 | async-start | bytes 524288 | tf_op jit(solution)/shard_map/all_to_all | solution.py:195
  101.8 4.8 %collective-permute-start.6 = (bf16[256,512]{1,0:T(8,128)(2,1)S(1)}, bf16[256,512]{1,0:T(8,128)(2,1)S(1)}, u32[]{:S(2)}, u32[]{:S(2)}) collective-permute-start(bf16[256,512]{1,0:T(8,128)(2,1)S(1)} %bitcast.17), channel_id=1, source_target_pairs={{0,8},{8,0},{16,24},{24,16},{32,40},{40,32},{48,56},{56,48},{64,72... | collective-permute-start | bytes 786440 | tf_op jit(solution)/shard_map/ppermute | solution.py:266

commit v2 on v1

v2 whole, which is shorter than its diff:
```python
import functools

import jax
import jax.numpy as jnp
from jax import lax
from jax.experimental import pallas as pl
from jax.experimental.pallas import tpu as pltpu
from jax.sharding import PartitionSpec as P

H = 64
KVH = 8
HD = 128
SPAN = 2048
CHUNK = 1024
STEP = 512
LOG2E = 1.4426950408889634
LARGE = 2.0**100
SMALL = 2.0**-60
ROWS_BY_ROWS = (((1,), (1,)), ((), ()))
VMEM = pl.BlockSpec(memory_space=pltpu.VMEM)
SMEM = pl.BlockSpec(memory_space=pltpu.SMEM)
HBM = pl.BlockSpec(memory_space=pltpu.HBM)
KERNEL = pltpu.CompilerParams(vmem_limit_bytes=32 * 2**20)


def core_of():
    return lax.rem(lax.axis_index("ctx"), 2)


def project_kernel(packed, hidden, query, key, value, out, sample):
    sample[...] = packed[:HD, -HD:]
    core = core_of()
    chips, rows, _ = out.shape
    width = query.shape[1]
    half = width // 2
    depth = hidden.shape[1]
    starts = [depth + core * half, depth + width + core * HD]
    own = [
        packed[:, pl.ds(pl.multiple_of(start, HD), size)]
        for start, size in zip(starts, (half, HD))
    ]

    def product(one, two):
        return (
            jnp.dot(packed[:, :depth], one, preferred_element_type=jnp.float32)
            + jnp.dot(hidden[...], two, preferred_element_type=jnp.float32)
        ).reshape(chips, rows, -1)

    columns = pl.ds(pl.multiple_of(core * half, half), half)
    out[:, :, :half] = product(own[0], query[:, columns])
    for index, weights in enumerate((key, value)):

        @pl.when(core == index)
        def _(weights=weights):
            out[:, :, half:] = product(own[1], weights[...])


def sum_kernel(width, pieces, queries, other):
    total = jnp.sum(pieces[...], axis=0)
    rows = (total[:, :width] * HD ** (-0.5)).astype(jnp.bfloat16)
    for place in range(queries.shape[0]):
        queries[place] = rows
    other[...] = total[:, width:].astype(jnp.bfloat16)


def three_parts(value):
    high = value.astype(jnp.bfloat16).astype(jnp.float32)
    rest = value - high
    middle = rest.astype(jnp.bfloat16).astype(jnp.float32)
    return (high, middle, rest - middle)


def attend_kernel(
    heads, count0, count1, queries, sample_keys, keys0, values0, keys1, values1, new_own,
    new_other, positions, out, keys, values, new_keys, new_values, stacked, reference, total,
    summed, arrivals,
):
    rows = queries.shape[0]
    block = keys0.shape[0]
    fetches = [
        pltpu.make_async_copy(
            source, target.at[pl.ds(index // 2 * block, block)], arrivals.at[index]
        )
        for index, (source, target) in enumerate(
            ((keys0, keys), (values0, values), (keys1, keys), (values1, values))
        )
    ]
    for fetch in fetches[:2]:
        fetch.start()
    lane = lax.broadcasted_iota(jnp.int32, (rows, HD), 1)
    count = new_own.shape[0]
    first = lax.axis_index("ctx") // 2 * count
    offset = lax.rem(first, HD)
    row_positions = jnp.transpose(jnp.broadcast_to(positions[...], (HD, rows)))
    key_positions = positions[:, pl.ds(pl.multiple_of(first - offset, HD), HD)]
    visible = (key_positions <= row_positions) & (lane >= offset) & (lane < offset + count)
    new_keys[...] = jnp.zeros_like(new_keys)
    new_values[...] = jnp.zeros_like(new_values)
    new_at = pl.ds(pl.multiple_of(offset, count), count)
    for index, pair in enumerate(((new_own, new_other), (new_other, new_own))):

        @pl.when(core_of() == index)
        def _(pair=pair):
            new_keys[new_at] = pair[0][...]
            new_values[new_at] = pair[1][...]

    def score(query, key):
        return lax.dot_general(
            query, key, ROWS_BY_ROWS, preferred_element_type=jnp.float32
        )

    sample = jnp.concatenate([sample_keys[...], new_keys[...]], axis=0)
    for head in range(heads):
        at = slice(head * rows, (head + 1) * rows)
        query = queries[:, head * HD : (head + 1) * HD]
        scores = score(query, sample)
        own = jnp.where(visible, scores[:, HD:], -jnp.inf)
        top = jnp.max(jnp.maximum(scores[:, :HD], own), axis=1, keepdims=True)
        level = jnp.broadcast_to(top, (rows, HD)).astype(jnp.bfloat16).astype(jnp.float32)
        stacked[at, :HD] = query
        stacked[at, HD:] = jnp.where(
            lane == 0, -level, jnp.where(lane == 1, 1.0, 0.0)
        ).astype(jnp.bfloat16)
        weights = jnp.exp2((own - level) * LOG2E)
        reference[at] = level
        total[at] = jnp.broadcast_to(jnp.sum(weights, axis=1, keepdims=True), (rows, HD))
        summed[at] = jnp.dot(
            weights.astype(jnp.bfloat16), new_values[...], preferred_element_type=jnp.float32
        )

    for fetch in fetches[2:]:
        fetch.start()
    span_lane = lax.broadcasted_iota(jnp.int32, (SPAN, HD), 1)

    def read_block(which, carry):
        for near in range(2):

            @pl.when(which == near)
            def _(near=near):
                fetches[2 * near].wait()
                fetches[2 * near + 1].wait()

        base = which * block
        limit = jnp.where(which == 0, count0[0], count1[0])

        def read_span(step, carry):
            start = pl.multiple_of(base + step * SPAN, SPAN)
            value = values[pl.ds(start, SPAN), :]
            place = step * SPAN + lax.broadcasted_iota(jnp.int32, (SPAN, HD), 0)
            bias = jnp.where(place < limit, 0.0, -1e30)
            extra = jnp.where(span_lane == 0, 1.0, jnp.where(span_lane == 1, bias, 0.0))
            key = jnp.concatenate(
                [keys[pl.ds(start, SPAN), :], extra.astype(jnp.bfloat16)], axis=1
            )
            for first_row in range(0, heads * rows, CHUNK):
                at = slice(first_row, first_row + CHUNK)
                scores = score(stacked[at], key)
                weights = jnp.exp2(scores * LOG2E)
                total[at] = total[at] + jnp.sum(weights, axis=1, keepdims=True)
                summed[at] = summed[at] + jnp.dot(
                    weights.astype(jnp.bfloat16), value, preferred_element_type=jnp.float32
                )
            return carry

        return lax.fori_loop(0, (limit + SPAN - 1) // SPAN, read_span, carry)

    lax.fori_loop(0, 2, read_block, 0)
    in_range = jnp.logical_and(jnp.max(total[...]) < LARGE, jnp.min(total[...]) > SMALL)

    @pl.when(jnp.logical_not(in_range))
    def _():
        reference[...] = jnp.full_like(reference, -jnp.inf)
        total[...] = jnp.zeros_like(total)
        summed[...] = jnp.zeros_like(summed)

        def update(at, scores, value):
            before = reference[at]
            now = jnp.maximum(before, jnp.max(scores, axis=1, keepdims=True))
            keep = jnp.exp(before - now)
            weights = jnp.exp(scores - now[:, :1])
            total[at] = total[at] * keep + jnp.sum(weights, axis=1, keepdims=True)
            summed[at] = summed[at] * keep + jnp.dot(
                weights.astype(jnp.bfloat16), value, preferred_element_type=jnp.float32
            )
            reference[at] = now

        def query_of(head):
            return queries[:, head * HD : (head + 1) * HD]

        def read_again(which, carry):
            base = which * block
            limit = jnp.where(which == 0, count0[0], count1[0])

            def read_step(step, carry):
                start = pl.multiple_of(base + step * STEP, STEP)
                place = step * STEP + lax.broadcasted_iota(jnp.int32, (1, STEP), 1)
                key = keys[pl.ds(start, STEP), :]
                value = values[pl.ds(start, STEP), :]
                for head in range(heads):
                    scores = jnp.where(place < limit, score(query_of(head), key), -jnp.inf)
                    update(slice(head * rows, (head + 1) * rows), scores, value)
                return carry

            return lax.fori_loop(0, (limit + STEP - 1) // STEP, read_step, carry)

        lax.fori_loop(0, 2, read_again, 0)
        for head in range(heads):
            scores = jnp.where(visible, score(query_of(head), new_keys[...]), -jnp.inf)
            update(slice(head * rows, (head + 1) * rows), scores, new_values[...])

    statistics = jnp.zeros((rows, HD), jnp.float32)
    for head in range(heads):
        at = slice(head * rows, (head + 1) * rows)
        out[:, head * HD : (head + 1) * HD] = summed[at].astype(jnp.bfloat16)
        parts = three_parts(reference[at]) + three_parts(total[at])
        for place, part in enumerate(parts):
            statistics = jnp.where(lane == 8 * head + place, part, statistics)
    out[:, heads * HD :] = statistics.astype(jnp.bfloat16)


def combine_kernel(heads, pieces, out):
    sources, rows, _ = pieces.shape
    width = heads * HD
    statistics = pieces[:, :, width:].reshape(sources * rows, HD)
    place = lax.broadcasted_iota(jnp.int32, (HD, width), 0)
    column = lax.broadcasted_iota(jnp.int32, (HD, width), 1)
    own = place // 8 == column // HD
    pick_top = jnp.where(own & (place % 8 < 3), 1.0, 0.0).astype(jnp.bfloat16)
    pick_total = jnp.where(own & (place % 8 >= 3) & (place % 8 < 6), 1.0, 0.0)
    tops = jnp.dot(statistics, pick_top, preferred_element_type=jnp.float32)
    totals = jnp.dot(
        statistics, pick_total.astype(jnp.bfloat16), preferred_element_type=jnp.float32
    )
    tops = tops.reshape(sources, rows, width)
    totals = totals.reshape(sources, rows, width)
    scale = jnp.exp(tops - jnp.max(tops, axis=0, keepdims=True))
    summed = jnp.sum(scale * pieces[:, :, :width].astype(jnp.float32), axis=0)
    context = (summed / jnp.sum(scale * totals, axis=0)).astype(jnp.bfloat16)
    for target in range(out.shape[0]):
        out[target] = context


def on_device(
    shards, hidden, w_query, w_key, w_value, w_out, key_cache, value_cache, block_count, positions
):
    query_count = hidden.shape[0]
    chips = shards // 2
    rows = query_count // chips
    half = w_query.shape[1] // 2
    heads = half // HD
    place = lax.axis_index("ctx")
    swap = [(index, index ^ 1) for index in range(shards)]
    same_core = [[2 * index + core for index in range(chips)] for core in range(2)]

    def exchange(array):
        return lax.all_to_all(array, "ctx", 0, 0, axis_index_groups=same_core)

    def swapped(array):
        return lax.ppermute(array, "ctx", swap)

    mine = (hidden, w_query, w_key, w_value)
    theirs = tuple(swapped(array) for array in mine)
    packed = jnp.concatenate(mine + (key_cache[: hidden.shape[0]],), axis=1)
    partial, sample_keys = pl.pallas_call(
        project_kernel,
        out_shape=(
            jax.ShapeDtypeStruct((chips, rows, half + HD), jnp.float32),
            jax.ShapeDtypeStruct((HD, HD), jnp.bfloat16),
        ),
        in_specs=[VMEM] * 5,
        out_specs=(VMEM, VMEM),
        compiler_params=KERNEL,
    )(packed, *theirs)
    partial, key_sent, value_sent = lax.optimization_barrier((partial, key_cache, value_cache))
    keys_other = swapped(key_sent)
    values_other = swapped(value_sent)
    pieces = exchange(partial)
    pieces, count_sent, places = lax.optimization_barrier((pieces, block_count, positions))
    count_other = swapped(count_sent)
    query_rows, new_own = pl.pallas_call(
        functools.partial(sum_kernel, half),
        out_shape=(
            jax.ShapeDtypeStruct((chips, rows, half), jnp.bfloat16),
            jax.ShapeDtypeStruct((rows, HD), jnp.bfloat16),
        ),
        in_specs=[VMEM],
        out_specs=(VMEM, VMEM),
        compiler_params=KERNEL,
    )(pieces)
    new_other = swapped(new_own)
    queries = exchange(query_rows).reshape(query_count, half)
    lanes = pltpu.VMEM((heads * query_count, HD), jnp.float32)
    local = pl.pallas_call(
        functools.partial(attend_kernel, heads),
        out_shape=jax.ShapeDtypeStruct((query_count, half + HD), jnp.bfloat16),
        in_specs=[SMEM] * 2 + [VMEM] * 2 + [HBM] * 4 + [VMEM] * 3,
        out_specs=VMEM,
        scratch_shapes=[
            pltpu.VMEM((2 * key_cache.shape[0], HD), jnp.bfloat16),
            pltpu.VMEM((2 * value_cache.shape[0], HD), jnp.bfloat16),
            pltpu.VMEM((HD, HD), jnp.bfloat16),
            pltpu.VMEM((HD, HD), jnp.bfloat16),
            pltpu.VMEM((heads * query_count, 2 * HD), jnp.bfloat16),
            lanes,
            lanes,
            lanes,
            pltpu.SemaphoreType.DMA((4,)),
        ],
        compiler_params=KERNEL,
    )(
        block_count,
        count_other,
        queries,
        sample_keys,
        key_cache,
        value_cache,
        keys_other,
        values_other,
        new_own,
        new_other,
        places.astype(jnp.float32)[None, :],
    )
    groups = exchange(local.reshape(chips, rows, half + HD))
    context_rows = pl.pallas_call(
        functools.partial(combine_kernel, heads),
        out_shape=jax.ShapeDtypeStruct((chips, rows, half), jnp.bfloat16),
        in_specs=[VMEM],
        out_specs=VMEM,
        compiler_params=KERNEL,
    )(groups)
    context = exchange(context_rows).reshape(query_count, half)
    context_other = lax.ppermute(context, "ctx", swap)
    start = (place % 2) * half
    out_own = lax.dynamic_slice_in_dim(w_out, start, half, 0)
    out_other = lax.dynamic_slice_in_dim(w_out, half - start, half, 0)
    attended = jnp.dot(context, out_own, preferred_element_type=jnp.float32) + jnp.dot(
        context_other, out_other, preferred_element_type=jnp.float32
    )
    parts = lax.axis_size("tp")
    attended = attended.astype(jnp.bfloat16).reshape(parts, query_count // parts, -1)
    received = lax.all_to_all(attended, "tp", 0, 0)
    return jnp.sum(received.astype(jnp.float32), axis=0).astype(jnp.bfloat16)


def solution(mesh):
    return jax.shard_map(
        functools.partial(on_device, mesh.shape["ctx"]),
        mesh=mesh,
        in_specs=(
            P(None, "ctx"),
            P("ctx", "tp"),
            P("ctx", "tp"),
            P("ctx", "tp"),
            P("tp", "ctx"),
            P("ctx", "tp"),
            P("ctx", "tp"),
            P("ctx"),
            P(),
        ),
        out_specs=P("tp", "ctx"),
        check_vma=False,
    )
```

time: 125 us -> 123 us (0.984); the launches traced: 123 us -> 124 us
  blocking collectives: 48.5 us -> 77.5 us
  waiting for transfers between devices: 18.1 us -> 5.91 us
  Pallas kernels: 29.5 us -> 21.7 us
  starting transfers between devices: 20 us -> 14.9 us
  other arithmetic: 3.5 us -> 0.63 us
  matrix products: 1.83 us -> 0.45 us
    all_to_all x2 -> x3, blocking collectives: 32.6 us -> 61.7 us  [exchange(): return lax.all_to_all(array, 'ctx', 0, 0, axis_index_groups=same_core)]
    all_to_all x2 -> x1, waiting for transfers between devices: 16.9 us -> 3.77 us  [exchange(): return lax.all_to_all(array, 'ctx', 0, 0, axis_index_groups=same_core)]
    pallas_call x1, Pallas kernels: 29.1 us -> 20 us  [on_device(): pl.pallas_call(functools.partial(attend_kernel, heads), out_shape=jax.Sha...]
    all_to_all x2 -> x1, starting transfers between devices: 8.68 us -> 3.54 us  [exchange(): return lax.all_to_all(array, 'ctx', 0, 0, axis_index_groups=same_core)]
    select_n x3 -> x0, other arithmetic: 2.08 us -> none  [the longest x1 1.19 us: on_device(): jnp.where(first, high, low)]
    dot_general x2 -> x0, matrix products: 1.37 us -> none  [the longest x1 1.11 us: on_device(): jnp.dot(hidden_other, columns_other, preferred_element_type=jnp.float32)]
    unnamed x12 -> x16, local copies, waits for them, and re-layouts: 0.73 us -> 2.1 us
    ppermute x6 -> x8, starting transfers between devices: 7.75 us -> 6.43 us  [swapped(): return lax.ppermute(array, 'ctx', swap)]
  transfers between devices with their start and end apart: 9 -> 10, of which waited for: 4 -> 3; matrix products, arithmetic and copies ran while one was open for 2% -> 2% of each run, Pallas kernels for 0% -> 1%
where the time goes in v2:
time: 123 us; the launch traced here: 124 us
  blocking collectives  77.5 us (63%)
  Pallas kernels  21.7 us (18%)
  starting transfers between devices  14.9 us (12%)
  waiting for transfers between devices  5.91 us (5%)
  local copies, waits for them, and re-layouts  2.12 us (2%)
    all_to_all x3, blocking collectives, exchange(): return lax.all_to_all(array, 'ctx', 0, 0, axis_index_groups=same_core)  61.7 us
    pallas_call x1, Pallas kernels, on_device(): pl.pallas_call(functools.partial(attend_kernel, heads), out_shape=jax.Sha...  20 us
    all_to_all x1, blocking collectives, on_device(): received = lax.all_to_all(attended, 'tp', 0, 0)  15.8 us
    ppermute x8, starting transfers between devices, swapped(): return lax.ppermute(array, 'ctx', swap)  6.43 us
    ppermute x1, starting transfers between devices, on_device(): context_other = lax.ppermute(context, 'ctx', swap)  4.9 us
    all_to_all x1, waiting for transfers between devices, exchange(): return lax.all_to_all(array, 'ctx', 0, 0, axis_index_groups=same_core)  3.77 us
    all_to_all x1, starting transfers between devices, exchange(): return lax.all_to_all(array, 'ctx', 0, 0, axis_index_groups=same_core)  3.54 us
  transfers between devices with their start and end apart: 10, of which 3 were waited for; matrix products, arithmetic and copies ran while one was open for 2% of the time, Pallas kernels for 1%

profile of v2, /device:TPU:1, one launch (start us, length us, event | category | flops | bytes accessed | tf_op | source)
XLA Modules:
  0.0 124.0 jit_solution(9751547925162589191)
XLA Ops:
  0.0 3.2 %collective-permute-start = (bf16[256,256]{1,0:T(8,128)(2,1)}, bf16[256,256]{1,0:T(8,128)(2,1)S(1)}, u32[]{:S(2)}, u32[]{:S(2)}) collective-permute-start(bf16[256,256]{1,0:T(8,128)(2,1)} %param.9), channel_id=1, source_target_pairs={{0,8},{8,0},{16,24},{24,16},{32,40},{40,32},{48,56},{56,48},{64,72... | collective-permute-start | bytes 393224 | tf_op jit(solution)/shard_map/ppermute | solution.py:259
  3.2 0.0 collective-permute-start.1
  3.2 0.5 collective-permute-start.2
  3.8 0.0 collective-permute-start.3
  3.8 0.9 constant_dynamic-update-slice_fusion.3
  4.7 0.0 copy-start.3
  4.7 0.0 copy-start.4
  4.7 1.1 constant_dynamic-update-slice_fusion.2
  5.8 0.0 copy-start.2
  5.9 0.0 collective-permute-done.2.key
  5.9 0.0 collective-permute-done.3.value
  6.0 0.5 shard_map.91
  6.5 0.6 collective-permute-start.5
  7.1 0.4 collective-permute-start.6
  7.6 17.1 %all_to_all.25.pieces = f32[16,16,640]{2,1,0:T(8,128)S(1)} all-to-all(f32[16,16,640]{2,1,0:T(8,128)S(1)} %get-tuple-element.16), channel_id=1, replica_groups={{0,16,32,48,64,80,96,112,128,144,160,176,192,208,224,240},{8,24,40,56,7..., dimensions={0} | all-to-all | bytes 1310720 | tf_op jit(solution)/shard_map/all_to_all | solution.py:256
  24.7 0.8 shard_map.92
  25.5 3.5 %all-to-all-start.1 = ((bf16[16,16,512]{2,1,0:T(8,128)(2,1)}), bf16[16,16,512]{2,1,0:T(8,128)(2,1)S(1)}, u32[]{:S(2)}, u32[]{:S(2)}) async-start(bf16[16,16,512]{2,1,0:T(8,128)(2,1)} %get-tuple-element.19), calls=%async_computation.1 | async-start | bytes 524288 | tf_op jit(solution)/shard_map/all_to_all | solution.py:256
  29.0 0.0 copy-start.5
  29.0 1.5 %collective-permute-start.7 = (bf16[16,128]{1,0:T(8,128)(2,1)S(1)}, bf16[16,128]{1,0:T(8,128)(2,1)S(1)}, u32[]{:S(2)}, u32[]{:S(2)}) collective-permute-start(bf16[16,128]{1,0:T(8,128)(2,1)S(1)} %get-tuple-element.23.new_own), channel_id=1, source_target_pairs={{0,8},{8,0},{16,24},{24,16},{32,40},{40,32},{48,56},{56,48},{64,72... | collective-permute-start | bytes 12296 | tf_op jit(solution)/shard_map/ppermute | solution.py:259
  31.2 0.1 collective-permute-start.4
  31.3 1.2 collective-permute-done.4.count1
  32.5 3.8 %all-to-all-done.1 = bf16[16,16,512]{2,1,0:T(8,128)(2,1)S(1)} async-done(((bf16[16,16,512]{2,1,0:T(8,128)(2,1)}), bf16[16,16,512]{2,1,0:T(8,128)(2,1)S(1)}, u32[]{:S(2)}, u32[]{:S(2)}) %all-to-all-start.1) | async-done | bytes 262176 | tf_op jit(solution)/shard_map/all_to_all | solution.py:256
  36.3 20.0 %shard_map.93 = bf16[256,640]{1,0:T(8,128)(2,1)S(1)} custom-call(s32[1]{0:T(128)S(6)} %copy.14.count0, s32[1]{0:T(128)} %collective-permute-done.4.count1, bf16[256,512]{1,0:T(8,128)(2,1)S(1)} %bitcast.8, bf16[128,128]{1,0:T(8,128)(2,1)S(1)} %get-tuple-element.20.sample_keys, bf16[4096,128]{1,0:T(8,128)(2,1)S(1)} %copy-done.1, ...), custom_call_target="tpu_custom_call" | custom-call | tf_op jit(solution)/shard_map/pallas_call | solution.py:293
  56.3 33.9 %all_to_all.26.pieces = bf16[16,16,640]{2,1,0:T(8,128)(2,1)S(1)} all-to-all(bf16[16,16,640]{2,1,0:T(8,128)(2,1)S(1)} %bitcast.7), channel_id=1, replica_groups={{0,16,32,48,64,80,96,112,128,144,160,176,192,208,224,240},{8,24,40,56,7..., dimensions={0} | all-to-all | bytes 655360 | tf_op jit(solution)/shard_map/all_to_all | solution.py:256
  90.2 0.4 shard_map.94
  90.6 10.7 %all_to_all.27 = bf16[16,16,512]{2,1,0:T(8,128)(2,1)S(1)} all-to-all(bf16[16,16,512]{2,1,0:T(8,128)(2,1)S(1)} %shard_map.94), channel_id=1, replica_groups={{0,16,32,48,64,80,96,112,128,144,160,176,192,208,224,240},{8,24,40,56,7..., dimensions={0} | all-to-all | bytes 524288 | tf_op jit(solution)/shard_map/all_to_all | solution.py:256
  101.3 4.9 %collective-permute-start.8 = (bf16[256,512]{1,0:T(8,128)(2,1)S(1)}, bf16[256,512]{1,0:T(8,128)(2,1)S(1)}, u32[]{:S(2)}, u32[]{:S(2)}) collective-permute-start(bf16[256,512]{1,0:T(8,128)(2,1)S(1)} %bitcast.10), channel_id=1, source_target_pairs={{0,8},{8,0},{16,24},{24,16},{32,40},{40,32},{48,56},{56,48},{64,72... | collective-permute-start | bytes 786440 | tf_op jit(solution)/shard_map/ppermute | solution.py:332
  106.2 0.2 fusion.2
  106.4 0.9 collective-permute-done.8
  107.3 0.2 fusion
  107.6 15.8 %all_to_all.28 = bf16[8,32,256]{2,1,0:T(8,128)(2,1)S(1)} all-to-all(bf16[8,32,256]{2,1,0:T(8,128)(2,1)S(1)} %bitcast.12), channel_id=1, replica_groups=mesh['ctx'=32,'tp'=8] {'tp'}, dimensions={0} | all-to-all | bytes 262144 | tf_op jit(solution)/shard_map/all_to_all | solution.py:341
  123.4 0.6 reduce_sum.12
  (17 shorter events, 0.1 us)
Async XLA Ops:
  0.0 106.2 %copy-start = (bf16[1024,256]{1,0:T(8,128)(2,1)S(1)}, bf16[1024,256]{1,0:T(8,128)(2,1)}, u32[]{:S(2)}) copy-start(bf16[1024,256]{1,0:T(8,128)(2,1)} %param.13) | copy-start | bytes 1572868
  0.0 5.9 %copy-start.1 = (bf16[4096,128]{1,0:T(8,128)(2,1)S(1)}, bf16[4096,128]{1,0:T(8,128)(2,1)}, u32[]{:S(2)}) copy-start(bf16[4096,128]{1,0:T(8,128)(2,1)} %keys0.1) | copy-start | bytes 3145732
  0.0 6.0 %collective-permute-start = (bf16[256,256]{1,0:T(8,128)(2,1)}, bf16[256,256]{1,0:T(8,128)(2,1)S(1)}, u32[]{:S(2)}, u32[]{:S(2)}) collective-permute-start(bf16[256,256]{1,0:T(8,128)(2,1)} %param.9), channel_id=1, source_target_pairs={{0,8},{8,0},{16,24},{24,16},{32,40},{40,32},{48,56},{56,48},{64,72... | collective-permute-start | bytes 393224 | tf_op jit(solution)/shard_map/ppermute | solution.py:259
  3.2 2.7 %collective-permute-start.1 = (bf16[256,1024]{1,0:T(8,128)(2,1)}, bf16[256,1024]{1,0:T(8,128)(2,1)S(1)}, u32[]{:S(2)}, u32[]{:S(2)}) collective-permute-start(bf16[256,1024]{1,0:T(8,128)(2,1)} %param.10), channel_id=1, source_target_pairs={{0,8},{8,0},{16,24},{24,16},{32,40},{40,32},{48,56},{56,48},{64,72... | collective-permute-start | bytes 1572872 | tf_op jit(solution)/shard_map/ppermute | solution.py:259
  3.2 2.7 %collective-permute-start.2 = (bf16[256,128]{1,0:T(8,128)(2,1)}, bf16[256,128]{1,0:T(8,128)(2,1)S(1)}, u32[]{:S(2)}, u32[]{:S(2)}) collective-permute-start(bf16[256,128]{1,0:T(8,128)(2,1)} %param.11), channel_id=1, source_target_pairs={{0,8},{8,0},{16,24},{24,16},{32,40},{40,32},{48,56},{56,48},{64,72... | collective-permute-start | bytes 196616 | tf_op jit(solution)/shard_map/ppermute | solution.py:259
  3.8 2.2 %collective-permute-start.3 = (bf16[256,128]{1,0:T(8,128)(2,1)}, bf16[256,128]{1,0:T(8,128)(2,1)S(1)}, u32[]{:S(2)}, u32[]{:S(2)}) collective-permute-start(bf16[256,128]{1,0:T(8,128)(2,1)} %param.12), channel_id=1, source_target_pairs={{0,8},{8,0},{16,24},{24,16},{32,40},{40,32},{48,56},{56,48},{64,72... | collective-permute-start | bytes 196616 | tf_op jit(solution)/shard_map/ppermute | solution.py:259
  4.7 1.1 copy-start.3
  4.7 1.2 copy-start.4
  5.8 1.3 %copy-start.2 = (bf16[4096,128]{1,0:T(8,128)(2,1)S(1)}, bf16[4096,128]{1,0:T(8,128)(2,1)}, u32[]{:S(2)}) copy-start(bf16[4096,128]{1,0:T(8,128)(2,1)} %values0.1) | copy-start | bytes 3145732
  6.5 29.8 %collective-permute-start.5 = (bf16[4096,128]{1,0:T(8,128)(2,1)S(1)}, bf16[4096,128]{1,0:T(8,128)(2,1)}, u32[]{:S(2)}, u32[]{:S(2)}) collective-permute-start(bf16[4096,128]{1,0:T(8,128)(2,1)S(1)} %copy-done.1), channel_id=1, source_target_pairs={{0,8},{8,0},{16,24},{24,16},{32,40},{40,32},{48,56},{56,48},{64,72... | collective-permute-start | bytes 3145736 | tf_op jit(solution)/shard_map/ppermute | solution.py:259
  7.1 29.2 %collective-permute-start.6 = (bf16[4096,128]{1,0:T(8,128)(2,1)S(1)}, bf16[4096,128]{1,0:T(8,128)(2,1)}, u32[]{:S(2)}, u32[]{:S(2)}) collective-permute-start(bf16[4096,128]{1,0:T(8,128)(2,1)S(1)} %copy-done.2), channel_id=1, source_target_pairs={{0,8},{8,0},{16,24},{24,16},{32,40},{40,32},{48,56},{56,48},{64,72... | collective-permute-start | bytes 3145736 | tf_op jit(solution)/shard_map/ppermute | solution.py:259
  25.5 10.9 %all-to-all-start.1 = ((bf16[16,16,512]{2,1,0:T(8,128)(2,1)}), bf16[16,16,512]{2,1,0:T(8,128)(2,1)S(1)}, u32[]{:S(2)}, u32[]{:S(2)}) async-start(bf16[16,16,512]{2,1,0:T(8,128)(2,1)} %get-tuple-element.19), calls=%async_computation.1 | async-start | bytes 524288 | tf_op jit(solution)/shard_map/all_to_all | solution.py:256
  29.0 2.3 %copy-start.5 = (s32[256]{0:T(256)S(1)}, s32[256]{0:T(256)}, u32[]{:S(2)}) copy-start(s32[256]{0:T(256)} %param.17) | copy-start | bytes 3076
  29.0 3.5 %collective-permute-start.7 = (bf16[16,128]{1,0:T(8,128)(2,1)S(1)}, bf16[16,128]{1,0:T(8,128)(2,1)S(1)}, u32[]{:S(2)}, u32[]{:S(2)}) collective-permute-start(bf16[16,128]{1,0:T(8,128)(2,1)S(1)} %get-tuple-element.23.new_own), channel_id=1, source_target_pairs={{0,8},{8,0},{16,24},{24,16},{32,40},{40,32},{48,56},{56,48},{64,72... | collective-permute-start | bytes 12296 | tf_op jit(solution)/shard_map/ppermute | solution.py:259
  31.2 1.3 %collective-permute-start.4 = (s32[1]{0:T(128)}, s32[1]{0:T(128)}, u32[]{:S(2)}, u32[]{:S(2)}) collective-permute-start(s32[1]{0:T(128)} %param.16), channel_id=1, source_target_pairs={{0,8},{8,0},{16,24},{24,16},{32,40},{40,32},{48,56},{56,48},{64,72... | collective-permute-start | bytes 20 | tf_op jit(solution)/shard_map/ppermute | solution.py:259
  101.3 6.1 %collective-permute-start.8 = (bf16[256,512]{1,0:T(8,128)(2,1)S(1)}, bf16[256,512]{1,0:T(8,128)(2,1)S(1)}, u32[]{:S(2)}, u32[]{:S(2)}) collective-permute-start(bf16[256,512]{1,0:T(8,128)(2,1)S(1)} %bitcast.10), channel_id=1, source_target_pairs={{0,8},{8,0},{16,24},{24,16},{32,40},{40,32},{48,56},{56,48},{64,72... | collective-permute-start | bytes 786440 | tf_op jit(solution)/shard_map/ppermute | solution.py:332

commit v3 on v2

--- a/solution.py
+++ b/solution.py
@@ -16,6 +16,7 @@
 LOG2E = 1.4426950408889634
 LARGE = 2.0**100
 SMALL = 2.0**-60
+RAISE = 32.0
 ROWS_BY_ROWS = (((1,), (1,)), ((), ()))
 VMEM = pl.BlockSpec(memory_space=pltpu.VMEM)
 SMEM = pl.BlockSpec(memory_space=pltpu.SMEM)
@@ -55,8 +56,8 @@
             out[:, :, half:] = product(own[1], weights[...])
 
 
-def sum_kernel(width, pieces, queries, other):
-    total = jnp.sum(pieces[...], axis=0)
+def spread_kernel(width, sums, queries, other):
+    total = sums[...]
     rows = (total[:, :width] * HD ** (-0.5)).astype(jnp.bfloat16)
     for place in range(queries.shape[0]):
         queries[place] = rows
@@ -274,11 +275,11 @@
     partial, key_sent, value_sent = lax.optimization_barrier((partial, key_cache, value_cache))
     keys_other = swapped(key_sent)
     values_other = swapped(value_sent)
-    pieces = exchange(partial)
+    pieces = exchange((partial * RAISE).astype(jnp.float16))
     pieces, count_sent, places = lax.optimization_barrier((pieces, block_count, positions))
     count_other = swapped(count_sent)
     query_rows, new_own = pl.pallas_call(
-        functools.partial(sum_kernel, half),
+        functools.partial(spread_kernel, half),
         out_shape=(
             jax.ShapeDtypeStruct((chips, rows, half), jnp.bfloat16),
             jax.ShapeDtypeStruct((rows, HD), jnp.bfloat16),
@@ -286,7 +287,7 @@
         in_specs=[VMEM],
         out_specs=(VMEM, VMEM),
         compiler_params=KERNEL,
-    )(pieces)
+    )(jnp.sum(pieces.astype(jnp.float32), axis=0) * (1.0 / RAISE))
     new_other = swapped(new_own)
     queries = exchange(query_rows).reshape(query_count, half)
     lanes = pltpu.VMEM((heads * query_count, HD), jnp.float32)

time: 123 us -> 117 us (0.951)
  blocking collectives: 77.5 us -> 50.1 us
  Pallas kernels: 21.7 us -> 41.2 us
    all_to_all x3, blocking collectives: 61.7 us -> 34.2 us  [exchange(): return lax.all_to_all(array, 'ctx', 0, 0, axis_index_groups=same_core)]
    pallas_call x1, Pallas kernels: 20 us -> 39.6 us  [on_device(): pl.pallas_call(functools.partial(attend_kernel, heads), out_shape=jax.Sha...]
where the time goes in v3:
time: 117 us
  blocking collectives  50.1 us (43%)
  Pallas kernels  41.2 us (35%)
  starting transfers between devices  15.4 us (13%)
  waiting for transfers between devices  5.91 us (5%)
  local copies, waits for them, and re-layouts  2.12 us (2%)
    pallas_call x1, Pallas kernels, on_device(): pl.pallas_call(functools.partial(attend_kernel, heads), out_shape=jax.Sha...  39.6 us
    all_to_all x3, blocking collectives, exchange(): return lax.all_to_all(array, 'ctx', 0, 0, axis_index_groups=same_core)  34.2 us
    all_to_all x1, blocking collectives, on_device(): received = lax.all_to_all(attended, 'tp', 0, 0)  15.9 us
    ppermute x8, starting transfers between devices, swapped(): return lax.ppermute(array, 'ctx', swap)  6.44 us
    ppermute x1, starting transfers between devices, on_device(): context_other = lax.ppermute(context, 'ctx', swap)  4.95 us
    all_to_all x1, starting transfers between devices, exchange(): return lax.all_to_all(array, 'ctx', 0, 0, axis_index_groups=same_core)  4.05 us
    all_to_all x1, waiting for transfers between devices, exchange(): return lax.all_to_all(array, 'ctx', 0, 0, axis_index_groups=same_core)  3.62 us
  transfers between devices with their start and end apart: 10, of which 3 were waited for; matrix products, arithmetic and copies ran while one was open for 2% of the time, Pallas kernels for 1%

profile of v3, /device:TPU:1, one launch (start us, length us, event | category | flops | bytes accessed | tf_op | source)
XLA Modules:
  0.0 116.8 jit_solution(15485480916156044082)
XLA Ops:
  0.0 3.2 %collective-permute-start = (bf16[256,256]{1,0:T(8,128)(2,1)}, bf16[256,256]{1,0:T(8,128)(2,1)S(1)}, u32[]{:S(2)}, u32[]{:S(2)}) collective-permute-start(bf16[256,256]{1,0:T(8,128)(2,1)} %param.9), channel_id=1, source_target_pairs={{0,8},{8,0},{16,24},{24,16},{32,40},{40,32},{48,56},{56,48},{64,72... | collective-permute-start | bytes 393224 | tf_op jit(solution)/shard_map/ppermute | solution.py:260
  3.2 0.0 collective-permute-start.1
  3.2 0.5 collective-permute-start.2
  3.8 0.0 collective-permute-start.3
  3.8 0.9 constant_dynamic-update-slice_fusion.3
  4.7 0.0 copy-start.3
  4.7 0.0 copy-start.4
  4.7 1.1 constant_dynamic-update-slice_fusion.2
  5.8 0.0 copy-start.2
  6.0 0.5 shard_map.91
  6.5 0.6 collective-permute-start.5
  7.1 0.4 collective-permute-start.6
  7.6 0.1 multiply_convert_fusion
  7.6 13.1 %all_to_all.25 = f16[16,16,640]{2,1,0:T(8,128)(2,1)S(1)} all-to-all(f16[16,16,640]{2,1,0:T(8,128)(2,1)S(1)} %multiply_convert_fusion), channel_id=1, replica_groups={{0,16,32,48,64,80,96,112,128,144,160,176,192,208,224,240},{8,24,40,56,7..., dimensions={0} | all-to-all | bytes 655360 | tf_op jit(solution)/shard_map/all_to_all | solution.py:257
  20.7 0.1 convert_reduce_fusion
  20.8 0.7 shard_map.92
  21.5 4.0 %all-to-all-start.1 = ((bf16[16,16,512]{2,1,0:T(8,128)(2,1)}), bf16[16,16,512]{2,1,0:T(8,128)(2,1)S(1)}, u32[]{:S(2)}, u32[]{:S(2)}) async-start(bf16[16,16,512]{2,1,0:T(8,128)(2,1)} %get-tuple-element.19), calls=%async_computation.1 | async-start | bytes 524288 | tf_op jit(solution)/shard_map/all_to_all | solution.py:257
  25.6 0.0 copy-start.5
  25.6 1.6 %collective-permute-start.7 = (bf16[16,128]{1,0:T(8,128)(2,1)S(1)}, bf16[16,128]{1,0:T(8,128)(2,1)S(1)}, u32[]{:S(2)}, u32[]{:S(2)}) collective-permute-start(bf16[16,128]{1,0:T(8,128)(2,1)S(1)} %get-tuple-element.23.new_own), channel_id=1, source_target_pairs={{0,8},{8,0},{16,24},{24,16},{32,40},{40,32},{48,56},{56,48},{64,72... | collective-permute-start | bytes 12296 | tf_op jit(solution)/shard_map/ppermute | solution.py:260
  27.8 0.1 collective-permute-start.4
  27.9 1.3 %collective-permute-done.4.count1 = s32[1]{0:T(128)} collective-permute-done((s32[1]{0:T(128)}, s32[1]{0:T(128)}, u32[]{:S(2)}, u32[]{:S(2)}) %collective-permute-start.4) | collective-permute-done | bytes 36 | tf_op jit(solution)/shard_map/ppermute | solution.py:260
  29.3 3.6 %all-to-all-done.1 = bf16[16,16,512]{2,1,0:T(8,128)(2,1)S(1)} async-done(((bf16[16,16,512]{2,1,0:T(8,128)(2,1)}), bf16[16,16,512]{2,1,0:T(8,128)(2,1)S(1)}, u32[]{:S(2)}, u32[]{:S(2)}) %all-to-all-start.1) | async-done | bytes 262176 | tf_op jit(solution)/shard_map/all_to_all | solution.py:257
  32.9 39.6 %shard_map.93 = bf16[256,640]{1,0:T(8,128)(2,1)S(1)} custom-call(s32[1]{0:T(128)S(6)} %copy.14.count0, s32[1]{0:T(128)} %collective-permute-done.4.count1, bf16[256,512]{1,0:T(8,128)(2,1)S(1)} %bitcast.8, bf16[128,128]{1,0:T(8,128)(2,1)S(1)} %get-tuple-element.20.sample_keys, bf16[4096,128]{1,0:T(8,128)(2,1)S(1)} %copy-done.1, ...), custom_call_target="tpu_custom_call" | custom-call | tf_op jit(solution)/shard_map/pallas_call | solution.py:294
  72.5 10.4 %all_to_all.26.pieces = bf16[16,16,640]{2,1,0:T(8,128)(2,1)S(1)} all-to-all(bf16[16,16,640]{2,1,0:T(8,128)(2,1)S(1)} %bitcast.7), channel_id=1, replica_groups={{0,16,32,48,64,80,96,112,128,144,160,176,192,208,224,240},{8,24,40,56,7..., dimensions={0} | all-to-all | bytes 655360 | tf_op jit(solution)/shard_map/all_to_all | solution.py:257
  82.9 0.4 shard_map.94
  83.3 10.7 %all_to_all.27 = bf16[16,16,512]{2,1,0:T(8,128)(2,1)S(1)} all-to-all(bf16[16,16,512]{2,1,0:T(8,128)(2,1)S(1)} %shard_map.94), channel_id=1, replica_groups={{0,16,32,48,64,80,96,112,128,144,160,176,192,208,224,240},{8,24,40,56,7..., dimensions={0} | all-to-all | bytes 524288 | tf_op jit(solution)/shard_map/all_to_all | solution.py:257
  94.0 4.9 %collective-permute-start.8 = (bf16[256,512]{1,0:T(8,128)(2,1)S(1)}, bf16[256,512]{1,0:T(8,128)(2,1)S(1)}, u32[]{:S(2)}, u32[]{:S(2)}) collective-permute-start(bf16[256,512]{1,0:T(8,128)(2,1)S(1)} %bitcast.10), channel_id=1, source_target_pairs={{0,8},{8,0},{16,24},{24,16},{32,40},{40,32},{48,56},{56,48},{64,72... | collective-permute-start | bytes 786440 | tf_op jit(solution)/shard_map/ppermute | solution.py:333
  98.9 0.2 fusion.2
  99.2 0.9 collective-permute-done.8
  100.1 0.2 fusion
  100.3 15.9 %all_to_all.28 = bf16[8,32,256]{2,1,0:T(8,128)(2,1)S(1)} all-to-all(bf16[8,32,256]{2,1,0:T(8,128)(2,1)S(1)} %bitcast.12), channel_id=1, replica_groups=mesh['ctx'=32,'tp'=8] {'tp'}, dimensions={0} | all-to-all | bytes 262144 | tf_op jit(solution)/shard_map/all_to_all | solution.py:342
  116.2 0.6 reduce_sum.22
  (20 shorter events, 0.1 us)
Async XLA Ops:
  0.0 98.9 %copy-start = (bf16[1024,256]{1,0:T(8,128)(2,1)S(1)}, bf16[1024,256]{1,0:T(8,128)(2,1)}, u32[]{:S(2)}) copy-start(bf16[1024,256]{1,0:T(8,128)(2,1)} %param.13) | copy-start | bytes 1572868
  0.0 5.9 %copy-start.1 = (bf16[4096,128]{1,0:T(8,128)(2,1)S(1)}, bf16[4096,128]{1,0:T(8,128)(2,1)}, u32[]{:S(2)}) copy-start(bf16[4096,128]{1,0:T(8,128)(2,1)} %keys0.1) | copy-start | bytes 3145732
  0.0 6.0 %collective-permute-start = (bf16[256,256]{1,0:T(8,128)(2,1)}, bf16[256,256]{1,0:T(8,128)(2,1)S(1)}, u32[]{:S(2)}, u32[]{:S(2)}) collective-permute-start(bf16[256,256]{1,0:T(8,128)(2,1)} %param.9), channel_id=1, source_target_pairs={{0,8},{8,0},{16,24},{24,16},{32,40},{40,32},{48,56},{56,48},{64,72... | collective-permute-start | bytes 393224 | tf_op jit(solution)/shard_map/ppermute | solution.py:260
  3.2 2.7 %collective-permute-start.1 = (bf16[256,1024]{1,0:T(8,128)(2,1)}, bf16[256,1024]{1,0:T(8,128)(2,1)S(1)}, u32[]{:S(2)}, u32[]{:S(2)}) collective-permute-start(bf16[256,1024]{1,0:T(8,128)(2,1)} %param.10), channel_id=1, source_target_pairs={{0,8},{8,0},{16,24},{24,16},{32,40},{40,32},{48,56},{56,48},{64,72... | collective-permute-start | bytes 1572872 | tf_op jit(solution)/shard_map/ppermute | solution.py:260
  3.2 2.7 %collective-permute-start.2 = (bf16[256,128]{1,0:T(8,128)(2,1)}, bf16[256,128]{1,0:T(8,128)(2,1)S(1)}, u32[]{:S(2)}, u32[]{:S(2)}) collective-permute-start(bf16[256,128]{1,0:T(8,128)(2,1)} %param.11), channel_id=1, source_target_pairs={{0,8},{8,0},{16,24},{24,16},{32,40},{40,32},{48,56},{56,48},{64,72... | collective-permute-start | bytes 196616 | tf_op jit(solution)/shard_map/ppermute | solution.py:260
  3.8 2.2 %collective-permute-start.3 = (bf16[256,128]{1,0:T(8,128)(2,1)}, bf16[256,128]{1,0:T(8,128)(2,1)S(1)}, u32[]{:S(2)}, u32[]{:S(2)}) collective-permute-start(bf16[256,128]{1,0:T(8,128)(2,1)} %param.12), channel_id=1, source_target_pairs={{0,8},{8,0},{16,24},{24,16},{32,40},{40,32},{48,56},{56,48},{64,72... | collective-permute-start | bytes 196616 | tf_op jit(solution)/shard_map/ppermute | solution.py:260
  4.7 1.1 copy-start.3
  4.7 1.2 %copy-start.4 = (bf16[256,128]{1,0:T(8,128)(2,1)S(1)}, bf16[256,128]{1,0:T(8,128)(2,1)}, u32[]{:S(2)}) copy-start(bf16[256,128]{1,0:T(8,128)(2,1)} %param.12) | copy-start | bytes 196612
  5.8 1.3 %copy-start.2 = (bf16[4096,128]{1,0:T(8,128)(2,1)S(1)}, bf16[4096,128]{1,0:T(8,128)(2,1)}, u32[]{:S(2)}) copy-start(bf16[4096,128]{1,0:T(8,128)(2,1)} %values0.1) | copy-start | bytes 3145732
  6.5 26.4 %collective-permute-start.5 = (bf16[4096,128]{1,0:T(8,128)(2,1)S(1)}, bf16[4096,128]{1,0:T(8,128)(2,1)}, u32[]{:S(2)}, u32[]{:S(2)}) collective-permute-start(bf16[4096,128]{1,0:T(8,128)(2,1)S(1)} %copy-done.1), channel_id=1, source_target_pairs={{0,8},{8,0},{16,24},{24,16},{32,40},{40,32},{48,56},{56,48},{64,72... | collective-permute-start | bytes 3145736 | tf_op jit(solution)/shard_map/ppermute | solution.py:260
  7.1 25.8 %collective-permute-start.6 = (bf16[4096,128]{1,0:T(8,128)(2,1)S(1)}, bf16[4096,128]{1,0:T(8,128)(2,1)}, u32[]{:S(2)}, u32[]{:S(2)}) collective-permute-start(bf16[4096,128]{1,0:T(8,128)(2,1)S(1)} %copy-done.2), channel_id=1, source_target_pairs={{0,8},{8,0},{16,24},{24,16},{32,40},{40,32},{48,56},{56,48},{64,72... | collective-permute-start | bytes 3145736 | tf_op jit(solution)/shard_map/ppermute | solution.py:260
  21.5 11.4 %all-to-all-start.1 = ((bf16[16,16,512]{2,1,0:T(8,128)(2,1)}), bf16[16,16,512]{2,1,0:T(8,128)(2,1)S(1)}, u32[]{:S(2)}, u32[]{:S(2)}) async-start(bf16[16,16,512]{2,1,0:T(8,128)(2,1)} %get-tuple-element.19), calls=%async_computation.1 | async-start | bytes 524288 | tf_op jit(solution)/shard_map/all_to_all | solution.py:257
  25.6 2.3 %copy-start.5 = (s32[256]{0:T(256)S(1)}, s32[256]{0:T(256)}, u32[]{:S(2)}) copy-start(s32[256]{0:T(256)} %param.17) | copy-start | bytes 3076
  25.6 3.7 %collective-permute-start.7 = (bf16[16,128]{1,0:T(8,128)(2,1)S(1)}, bf16[16,128]{1,0:T(8,128)(2,1)S(1)}, u32[]{:S(2)}, u32[]{:S(2)}) collective-permute-start(bf16[16,128]{1,0:T(8,128)(2,1)S(1)} %get-tuple-element.23.new_own), channel_id=1, source_target_pairs={{0,8},{8,0},{16,24},{24,16},{32,40},{40,32},{48,56},{56,48},{64,72... | collective-permute-start | bytes 12296 | tf_op jit(solution)/shard_map/ppermute | solution.py:260
  27.8 1.5 %collective-permute-start.4 = (s32[1]{0:T(128)}, s32[1]{0:T(128)}, u32[]{:S(2)}, u32[]{:S(2)}) collective-permute-start(s32[1]{0:T(128)} %param.16), channel_id=1, source_target_pairs={{0,8},{8,0},{16,24},{24,16},{32,40},{40,32},{48,56},{56,48},{64,72... | collective-permute-start | bytes 20 | tf_op jit(solution)/shard_map/ppermute | solution.py:260
  94.0 6.1 %collective-permute-start.8 = (bf16[256,512]{1,0:T(8,128)(2,1)S(1)}, bf16[256,512]{1,0:T(8,128)(2,1)S(1)}, u32[]{:S(2)}, u32[]{:S(2)}) collective-permute-start(bf16[256,512]{1,0:T(8,128)(2,1)S(1)} %bitcast.10), channel_id=1, source_target_pairs={{0,8},{8,0},{16,24},{24,16},{32,40},{40,32},{48,56},{56,48},{64,72... | collective-permute-start | bytes 786440 | tf_op jit(solution)/shard_map/ppermute | solution.py:333

commit v4 on v3

--- a/solution.py
+++ b/solution.py
@@ -28,14 +28,12 @@
     return lax.rem(lax.axis_index("ctx"), 2)
 
 
-def project_kernel(packed, hidden, query, key, value, out, sample):
-    sample[...] = packed[:HD, -HD:]
+def project_kernel(hidden_own, packed, hidden, query, key, value, out):
     core = core_of()
     chips, rows, _ = out.shape
     width = query.shape[1]
     half = width // 2
-    depth = hidden.shape[1]
-    starts = [depth + core * half, depth + width + core * HD]
+    starts = [core * half, width + core * HD]
     own = [
         packed[:, pl.ds(pl.multiple_of(start, HD), size)]
         for start, size in zip(starts, (half, HD))
@@ -43,7 +41,7 @@
 
     def product(one, two):
         return (
-            jnp.dot(packed[:, :depth], one, preferred_element_type=jnp.float32)
+            jnp.dot(hidden_own[...], one, preferred_element_type=jnp.float32)
             + jnp.dot(hidden[...], two, preferred_element_type=jnp.float32)
         ).reshape(chips, rows, -1)
 
@@ -261,20 +259,14 @@
 
     mine = (hidden, w_query, w_key, w_value)
     theirs = tuple(swapped(array) for array in mine)
-    packed = jnp.concatenate(mine + (key_cache[: hidden.shape[0]],), axis=1)
-    partial, sample_keys = pl.pallas_call(
+    packed = jnp.concatenate(mine[1:], axis=1)
+    partial = pl.pallas_call(
         project_kernel,
-        out_shape=(
-            jax.ShapeDtypeStruct((chips, rows, half + HD), jnp.float32),
-            jax.ShapeDtypeStruct((HD, HD), jnp.bfloat16),
-        ),
-        in_specs=[VMEM] * 5,
-        out_specs=(VMEM, VMEM),
+        out_shape=jax.ShapeDtypeStruct((chips, rows, half + HD), jnp.float32),
+        in_specs=[VMEM] * 6,
+        out_specs=VMEM,
         compiler_params=KERNEL,
-    )(packed, *theirs)
-    partial, key_sent, value_sent = lax.optimization_barrier((partial, key_cache, value_cache))
-    keys_other = swapped(key_sent)
-    values_other = swapped(value_sent)
+    )(hidden, packed, *theirs)
     pieces = exchange((partial * RAISE).astype(jnp.float16))
     pieces, count_sent, places = lax.optimization_barrier((pieces, block_count, positions))
     count_other = swapped(count_sent)
@@ -288,6 +280,10 @@
         out_specs=(VMEM, VMEM),
         compiler_params=KERNEL,
     )(jnp.sum(pieces.astype(jnp.float32), axis=0) * (1.0 / RAISE))
+    new_own, key_sent, value_sent = lax.optimization_barrier((new_own, key_cache, value_cache))
+    sample_keys = key_sent[:HD]
+    keys_other = swapped(key_sent)
+    values_other = swapped(value_sent)
     new_other = swapped(new_own)
     queries = exchange(query_rows).reshape(query_count, half)
     lanes = pltpu.VMEM((heads * query_count, HD), jnp.float32)

time: 117 us -> 119 us (1.017)
  blocking collectives: 50.1 us -> 59.1 us
  Pallas kernels: 41.2 us -> 33.9 us
  local copies, waits for them, and re-layouts: 2.12 us -> 0.03 us
  waiting for transfers between devices: 5.91 us -> 7.46 us
    all_to_all x3, blocking collectives: 34.2 us -> 43.2 us  [exchange(): return lax.all_to_all(array, 'ctx', 0, 0, axis_index_groups=same_core)]
    pallas_call x1, Pallas kernels: 39.6 us -> 32.3 us  [on_device(): pl.pallas_call(functools.partial(attend_kernel, heads), out_shape=jax.Sha...]
    unnamed x16 -> x10, local copies, waits for them, and re-layouts: 2.1 us -> 0.03 us
    all_to_all x1, waiting for transfers between devices: 3.62 us -> 4.9 us  [exchange(): return lax.all_to_all(array, 'ctx', 0, 0, axis_index_groups=same_core)]
  transfers between devices with their start and end apart: 10 -> 10, of which waited for: 3 -> 5; matrix products, arithmetic and copies ran while one was open for 2% -> 1% of each run, Pallas kernels for 1% -> 0%
where the time goes in v4:
time: 119 us; the launch traced here: 118 us
  blocking collectives  59.1 us (50%)
  Pallas kernels  33.9 us (28%)
  starting transfers between devices  14.5 us (12%)
  waiting for transfers between devices  7.46 us (6%)
  other arithmetic  1.92 us (2%)
    all_to_all x3, blocking collectives, exchange(): return lax.all_to_all(array, 'ctx', 0, 0, axis_index_groups=same_core)  43.2 us
    pallas_call x1, Pallas kernels, on_device(): pl.pallas_call(functools.partial(attend_kernel, heads), out_shape=jax.Sha...  32.3 us
    all_to_all x1, blocking collectives, on_device(): received = lax.all_to_all(attended, 'tp', 0, 0)  15.9 us
    ppermute x8, starting transfers between devices, swapped(): return lax.ppermute(array, 'ctx', swap)  6.75 us
    all_to_all x1, waiting for transfers between devices, exchange(): return lax.all_to_all(array, 'ctx', 0, 0, axis_index_groups=same_core)  4.9 us
    ppermute x1, starting transfers between devices, on_device(): context_other = lax.ppermute(context, 'ctx', swap)  4.23 us
    all_to_all x1, starting transfers between devices, exchange(): return lax.all_to_all(array, 'ctx', 0, 0, axis_index_groups=same_core)  3.53 us
  transfers between devices with their start and end apart: 10, of which 5 were waited for; matrix products, arithmetic and copies ran while one was open for 1% of the time, Pallas kernels for 0%

profile of v4, /device:TPU:1, one launch (start us, length us, event | category | flops | bytes accessed | tf_op | source)
XLA Modules:
  0.0 118.1 jit_solution(11881005519132912901)
XLA Ops:
  0.0 3.2 %collective-permute-start.1 = (bf16[256,1024]{1,0:T(8,128)(2,1)}, bf16[256,1024]{1,0:T(8,128)(2,1)S(1)}, u32[]{:S(2)}, u32[]{:S(2)}) collective-permute-start(bf16[256,1024]{1,0:T(8,128)(2,1)} %param.10), channel_id=1, source_target_pairs={{0,8},{8,0},{16,24},{24,16},{32,40},{40,32},{48,56},{56,48},{64,72... | collective-permute-start | bytes 1572872 | tf_op jit(solution)/shard_map/ppermute | solution.py:258
  3.2 0.0 collective-permute-start
  3.2 0.5 collective-permute-start.2
  3.8 0.0 collective-permute-start.3
  3.8 1.2 pad_maximum_fusion.packed
  4.9 0.3 collective-permute-done.2.key
  5.3 0.1 collective-permute-done.3.value
  5.4 0.5 shard_map.91
  5.9 0.0 copy-start.1
  5.9 0.0 copy-start.2
  5.9 0.1 multiply_convert_fusion
  6.0 0.0 copy-start.4
  6.0 12.9 %all_to_all.25 = f16[16,16,640]{2,1,0:T(8,128)(2,1)S(1)} all-to-all(f16[16,16,640]{2,1,0:T(8,128)(2,1)S(1)} %multiply_convert_fusion), channel_id=1, replica_groups={{0,16,32,48,64,80,96,112,128,144,160,176,192,208,224,240},{8,24,40,56,7..., dimensions={0} | all-to-all | bytes 655360 | tf_op jit(solution)/shard_map/all_to_all | solution.py:255
  18.9 0.1 convert_reduce_fusion
  19.0 0.7 shard_map.92
  19.7 2.2 %collective-permute-start.5 = (bf16[4096,128]{1,0:T(8,128)(2,1)S(1)}, bf16[4096,128]{1,0:T(8,128)(2,1)}, u32[]{:S(2)}, u32[]{:S(2)}) collective-permute-start(bf16[4096,128]{1,0:T(8,128)(2,1)S(1)} %copy-done.1), channel_id=1, source_target_pairs={{0,8},{8,0},{16,24},{24,16},{32,40},{40,32},{48,56},{56,48},{64,72... | collective-permute-start | bytes 3145736 | tf_op jit(solution)/shard_map/ppermute | solution.py:258
  21.9 0.1 collective-permute-start.6
  22.0 3.5 %all-to-all-start.1 = ((bf16[16,16,512]{2,1,0:T(8,128)(2,1)}), bf16[16,16,512]{2,1,0:T(8,128)(2,1)S(1)}, u32[]{:S(2)}, u32[]{:S(2)}) async-start(bf16[16,16,512]{2,1,0:T(8,128)(2,1)} %get-tuple-element.15), calls=%async_computation.1 | async-start | bytes 524288 | tf_op jit(solution)/shard_map/all_to_all | solution.py:255
  25.5 0.6 collective-permute-start.7
  26.8 0.1 collective-permute-start.4
  27.0 1.2 %collective-permute-done.4.count1 = s32[1]{0:T(128)} collective-permute-done((s32[1]{0:T(128)}, s32[1]{0:T(128)}, u32[]{:S(2)}, u32[]{:S(2)}) %collective-permute-start.4) | collective-permute-done | bytes 36 | tf_op jit(solution)/shard_map/ppermute | solution.py:258
  28.2 4.9 %all-to-all-done.1 = bf16[16,16,512]{2,1,0:T(8,128)(2,1)S(1)} async-done(((bf16[16,16,512]{2,1,0:T(8,128)(2,1)}), bf16[16,16,512]{2,1,0:T(8,128)(2,1)S(1)}, u32[]{:S(2)}, u32[]{:S(2)}) %all-to-all-start.1) | async-done | bytes 262176 | tf_op jit(solution)/shard_map/all_to_all | solution.py:255
  33.1 32.3 %shard_map.93 = bf16[256,640]{1,0:T(8,128)(2,1)S(1)} custom-call(s32[1]{0:T(128)S(6)} %copy.10.count0, s32[1]{0:T(128)} %collective-permute-done.4.count1, bf16[256,512]{1,0:T(8,128)(2,1)S(1)} %bitcast.8, bf16[128,128]{1,0:T(8,128)(2,1)S(1)} %slice.3.sample_keys, bf16[4096,128]{1,0:T(8,128)(2,1)S(1)} %copy-done.1, bf16[4096,128]{1,0:T(8,128)(2,1)S(1)} %copy-done.2, ...), custom_call_target="tpu_custom_call" | custom-call | tf_op jit(solution)/shard_map/pallas_call | solution.py:290
  65.3 19.5 %all_to_all.26.pieces = bf16[16,16,640]{2,1,0:T(8,128)(2,1)S(1)} all-to-all(bf16[16,16,640]{2,1,0:T(8,128)(2,1)S(1)} %bitcast.7), channel_id=1, replica_groups={{0,16,32,48,64,80,96,112,128,144,160,176,192,208,224,240},{8,24,40,56,7..., dimensions={0} | all-to-all | bytes 655360 | tf_op jit(solution)/shard_map/all_to_all | solution.py:255
  84.8 0.4 shard_map.94
  85.2 10.8 %all_to_all.27 = bf16[16,16,512]{2,1,0:T(8,128)(2,1)S(1)} all-to-all(bf16[16,16,512]{2,1,0:T(8,128)(2,1)S(1)} %shard_map.94), channel_id=1, replica_groups={{0,16,32,48,64,80,96,112,128,144,160,176,192,208,224,240},{8,24,40,56,7..., dimensions={0} | all-to-all | bytes 524288 | tf_op jit(solution)/shard_map/all_to_all | solution.py:255
  96.0 4.2 %collective-permute-start.8 = (bf16[256,512]{1,0:T(8,128)(2,1)S(1)}, bf16[256,512]{1,0:T(8,128)(2,1)S(1)}, u32[]{:S(2)}, u32[]{:S(2)}) collective-permute-start(bf16[256,512]{1,0:T(8,128)(2,1)S(1)} %bitcast.10), channel_id=1, source_target_pairs={{0,8},{8,0},{16,24},{24,16},{32,40},{40,32},{48,56},{56,48},{64,72... | collective-permute-start | bytes 786440 | tf_op jit(solution)/shard_map/ppermute | solution.py:329
  100.3 0.2 fusion.2
  100.5 0.9 collective-permute-done.8
  101.4 0.2 fusion
  101.6 15.9 %all_to_all.28 = bf16[8,32,256]{2,1,0:T(8,128)(2,1)S(1)} all-to-all(bf16[8,32,256]{2,1,0:T(8,128)(2,1)S(1)} %bitcast.12), channel_id=1, replica_groups=mesh['ctx'=32,'tp'=8] {'tp'}, dimensions={0} | all-to-all | bytes 262144 | tf_op jit(solution)/shard_map/all_to_all | solution.py:338
  117.5 0.6 reduce_sum.22
  (15 shorter events, 0.0 us)
Async XLA Ops:
  0.0 100.3 %copy-start = (bf16[1024,256]{1,0:T(8,128)(2,1)S(1)}, bf16[1024,256]{1,0:T(8,128)(2,1)}, u32[]{:S(2)}) copy-start(bf16[1024,256]{1,0:T(8,128)(2,1)} %param.13) | copy-start | bytes 1572868
  0.0 5.4 %copy-start.3 = (bf16[256,256]{1,0:T(8,128)(2,1)S(1)}, bf16[256,256]{1,0:T(8,128)(2,1)}, u32[]{:S(2)}) copy-start(bf16[256,256]{1,0:T(8,128)(2,1)} %hidden_own.1) | copy-start | bytes 393220
  0.0 5.4 %collective-permute-start.1 = (bf16[256,1024]{1,0:T(8,128)(2,1)}, bf16[256,1024]{1,0:T(8,128)(2,1)S(1)}, u32[]{:S(2)}, u32[]{:S(2)}) collective-permute-start(bf16[256,1024]{1,0:T(8,128)(2,1)} %param.10), channel_id=1, source_target_pairs={{0,8},{8,0},{16,24},{24,16},{32,40},{40,32},{48,56},{56,48},{64,72... | collective-permute-start | bytes 1572872 | tf_op jit(solution)/shard_map/ppermute | solution.py:258
  3.2 2.1 %collective-permute-start = (bf16[256,256]{1,0:T(8,128)(2,1)}, bf16[256,256]{1,0:T(8,128)(2,1)S(1)}, u32[]{:S(2)}, u32[]{:S(2)}) collective-permute-start(bf16[256,256]{1,0:T(8,128)(2,1)} %hidden_own.1), channel_id=1, source_target_pairs={{0,8},{8,0},{16,24},{24,16},{32,40},{40,32},{48,56},{56,48},{64,72... | collective-permute-start | bytes 393224 | tf_op jit(solution)/shard_map/ppermute | solution.py:258
  3.2 2.0 %collective-permute-start.2 = (bf16[256,128]{1,0:T(8,128)(2,1)}, bf16[256,128]{1,0:T(8,128)(2,1)S(1)}, u32[]{:S(2)}, u32[]{:S(2)}) collective-permute-start(bf16[256,128]{1,0:T(8,128)(2,1)} %param.11), channel_id=1, source_target_pairs={{0,8},{8,0},{16,24},{24,16},{32,40},{40,32},{48,56},{56,48},{64,72... | collective-permute-start | bytes 196616 | tf_op jit(solution)/shard_map/ppermute | solution.py:258
  3.8 1.6 %collective-permute-start.3 = (bf16[256,128]{1,0:T(8,128)(2,1)}, bf16[256,128]{1,0:T(8,128)(2,1)S(1)}, u32[]{:S(2)}, u32[]{:S(2)}) collective-permute-start(bf16[256,128]{1,0:T(8,128)(2,1)} %param.12), channel_id=1, source_target_pairs={{0,8},{8,0},{16,24},{24,16},{32,40},{40,32},{48,56},{56,48},{64,72... | collective-permute-start | bytes 196616 | tf_op jit(solution)/shard_map/ppermute | solution.py:258
  5.9 13.8 %copy-start.1 = (bf16[4096,128]{1,0:T(8,128)(2,1)S(1)}, bf16[4096,128]{1,0:T(8,128)(2,1)}, u32[]{:S(2)}) copy-start(bf16[4096,128]{1,0:T(8,128)(2,1)} %keys0.1) | copy-start | bytes 3145732
  5.9 16.0 %copy-start.2 = (bf16[4096,128]{1,0:T(8,128)(2,1)S(1)}, bf16[4096,128]{1,0:T(8,128)(2,1)}, u32[]{:S(2)}) copy-start(bf16[4096,128]{1,0:T(8,128)(2,1)} %values0.1) | copy-start | bytes 3145732
  6.0 20.9 %copy-start.4 = (s32[256]{0:T(256)S(1)}, s32[256]{0:T(256)}, u32[]{:S(2)}) copy-start(s32[256]{0:T(256)} %param.17) | copy-start | bytes 3076
  19.7 13.3 %collective-permute-start.5 = (bf16[4096,128]{1,0:T(8,128)(2,1)S(1)}, bf16[4096,128]{1,0:T(8,128)(2,1)}, u32[]{:S(2)}, u32[]{:S(2)}) collective-permute-start(bf16[4096,128]{1,0:T(8,128)(2,1)S(1)} %copy-done.1), channel_id=1, source_target_pairs={{0,8},{8,0},{16,24},{24,16},{32,40},{40,32},{48,56},{56,48},{64,72... | collective-permute-start | bytes 3145736 | tf_op jit(solution)/shard_map/ppermute | solution.py:258
  21.9 11.2 %collective-permute-start.6 = (bf16[4096,128]{1,0:T(8,128)(2,1)S(1)}, bf16[4096,128]{1,0:T(8,128)(2,1)}, u32[]{:S(2)}, u32[]{:S(2)}) collective-permute-start(bf16[4096,128]{1,0:T(8,128)(2,1)S(1)} %copy-done.2), channel_id=1, source_target_pairs={{0,8},{8,0},{16,24},{24,16},{32,40},{40,32},{48,56},{56,48},{64,72... | collective-permute-start | bytes 3145736 | tf_op jit(solution)/shard_map/ppermute | solution.py:258
  22.0 11.1 %all-to-all-start.1 = ((bf16[16,16,512]{2,1,0:T(8,128)(2,1)}), bf16[16,16,512]{2,1,0:T(8,128)(2,1)S(1)}, u32[]{:S(2)}, u32[]{:S(2)}) async-start(bf16[16,16,512]{2,1,0:T(8,128)(2,1)} %get-tuple-element.15), calls=%async_computation.1 | async-start | bytes 524288 | tf_op jit(solution)/shard_map/all_to_all | solution.py:255
  25.5 2.6 %collective-permute-start.7 = (bf16[16,128]{1,0:T(8,128)(2,1)S(1)}, bf16[16,128]{1,0:T(8,128)(2,1)S(1)}, u32[]{:S(2)}, u32[]{:S(2)}) collective-permute-start(bf16[16,128]{1,0:T(8,128)(2,1)S(1)} %get-tuple-element.19.new_own), channel_id=1, source_target_pairs={{0,8},{8,0},{16,24},{24,16},{32,40},{40,32},{48,56},{56,48},{64,72... | collective-permute-start | bytes 12296 | tf_op jit(solution)/shard_map/ppermute | solution.py:258
  26.8 1.3 %collective-permute-start.4 = (s32[1]{0:T(128)}, s32[1]{0:T(128)}, u32[]{:S(2)}, u32[]{:S(2)}) collective-permute-start(s32[1]{0:T(128)} %param.16), channel_id=1, source_target_pairs={{0,8},{8,0},{16,24},{24,16},{32,40},{40,32},{48,56},{56,48},{64,72... | collective-permute-start | bytes 20 | tf_op jit(solution)/shard_map/ppermute | solution.py:258
  96.0 5.4 %collective-permute-start.8 = (bf16[256,512]{1,0:T(8,128)(2,1)S(1)}, bf16[256,512]{1,0:T(8,128)(2,1)S(1)}, u32[]{:S(2)}, u32[]{:S(2)}) collective-permute-start(bf16[256,512]{1,0:T(8,128)(2,1)S(1)} %bitcast.10), channel_id=1, source_target_pairs={{0,8},{8,0},{16,24},{24,16},{32,40},{40,32},{48,56},{56,48},{64,72... | collective-permute-start | bytes 786440 | tf_op jit(solution)/shard_map/ppermute | solution.py:329

commit v5 on v4

--- a/solution.py
+++ b/solution.py
@@ -239,6 +239,10 @@
         out[target] = context
 
 
+def total_kernel(pieces, out):
+    out[...] = jnp.sum(pieces[...].astype(jnp.float32), axis=0).astype(jnp.bfloat16)
+
+
 def on_device(
     shards, hidden, w_query, w_key, w_value, w_out, key_cache, value_cache, block_count, positions
 ):
@@ -336,7 +340,13 @@
     parts = lax.axis_size("tp")
     attended = attended.astype(jnp.bfloat16).reshape(parts, query_count // parts, -1)
     received = lax.all_to_all(attended, "tp", 0, 0)
-    return jnp.sum(received.astype(jnp.float32), axis=0).astype(jnp.bfloat16)
+    return pl.pallas_call(
+        total_kernel,
+        out_shape=jax.ShapeDtypeStruct(received.shape[1:], jnp.bfloat16),
+        in_specs=[VMEM],
+        out_specs=VMEM,
+        compiler_params=KERNEL,
+    )(received)
 
 
 def solution(mesh):

time: 119 us -> 120 us (level)
  Pallas kernels: 33.9 us -> 40.2 us
  blocking collectives: 59.1 us -> 55.5 us
    pallas_call x1, Pallas kernels: 32.3 us -> 37.9 us  [on_device(): pl.pallas_call(functools.partial(attend_kernel, heads), out_shape=jax.Sha...]
    all_to_all x3, blocking collectives: 43.2 us -> 39.6 us  [exchange(): return lax.all_to_all(array, 'ctx', 0, 0, axis_index_groups=same_core)]
where the time goes in v5:
time: 120 us
  blocking collectives  55.5 us (46%)
  Pallas kernels  40.2 us (34%)
  starting transfers between devices  14.1 us (12%)
  waiting for transfers between devices  7.46 us (6%)
  other arithmetic  1.29 us (1%)
    all_to_all x3, blocking collectives, exchange(): return lax.all_to_all(array, 'ctx', 0, 0, axis_index_groups=same_core)  39.6 us
    pallas_call x1, Pallas kernels, on_device(): pl.pallas_call(functools.partial(attend_kernel, heads), out_shape=jax.Sha...  37.9 us
    all_to_all x1, blocking collectives, on_device(): received = lax.all_to_all(attended, 'tp', 0, 0)  15.9 us
    ppermute x8, starting transfers between devices, swapped(): return lax.ppermute(array, 'ctx', swap)  6.75 us
    all_to_all x1, waiting for transfers between devices, exchange(): return lax.all_to_all(array, 'ctx', 0, 0, axis_index_groups=same_core)  4.9 us
    ppermute x1, starting transfers between devices, on_device(): context_other = lax.ppermute(context, 'ctx', swap)  3.84 us
    all_to_all x1, starting transfers between devices, exchange(): return lax.all_to_all(array, 'ctx', 0, 0, axis_index_groups=same_core)  3.53 us
  transfers between devices with their start and end apart: 10, of which 5 were waited for; matrix products, arithmetic and copies ran while one was open for 1% of the time, Pallas kernels for 0%

profile of v5, /device:TPU:1, one launch (start us, length us, event | category | flops | bytes accessed | tf_op | source)
XLA Modules:
  0.0 119.8 jit_solution(6490803235866033930)
XLA Ops:
  0.0 3.2 %collective-permute-start.1 = (bf16[256,1024]{1,0:T(8,128)(2,1)}, bf16[256,1024]{1,0:T(8,128)(2,1)S(1)}, u32[]{:S(2)}, u32[]{:S(2)}) collective-permute-start(bf16[256,1024]{1,0:T(8,128)(2,1)} %param.10), channel_id=1, source_target_pairs={{0,8},{8,0},{16,24},{24,16},{32,40},{40,32},{48,56},{56,48},{64,72... | collective-permute-start | bytes 1572872 | tf_op jit(solution)/shard_map/ppermute | solution.py:262
  3.2 0.0 collective-permute-start
  3.2 0.5 collective-permute-start.2
  3.8 0.0 collective-permute-start.3
  3.8 1.2 pad_maximum_fusion.packed
  4.9 0.3 collective-permute-done.2.key
  5.3 0.1 collective-permute-done.3.value
  5.4 0.5 shard_map.91
  5.9 0.0 copy-start.1
  5.9 0.0 copy-start.2
  5.9 0.1 multiply_convert_fusion
  6.0 0.0 copy-start.4
  6.0 12.9 %all_to_all.25 = f16[16,16,640]{2,1,0:T(8,128)(2,1)S(1)} all-to-all(f16[16,16,640]{2,1,0:T(8,128)(2,1)S(1)} %multiply_convert_fusion), channel_id=1, replica_groups={{0,16,32,48,64,80,96,112,128,144,160,176,192,208,224,240},{8,24,40,56,7..., dimensions={0} | all-to-all | bytes 655360 | tf_op jit(solution)/shard_map/all_to_all | solution.py:259
  18.9 0.1 convert_reduce_fusion
  19.0 0.7 shard_map.92
  19.7 2.2 %collective-permute-start.5 = (bf16[4096,128]{1,0:T(8,128)(2,1)S(1)}, bf16[4096,128]{1,0:T(8,128)(2,1)}, u32[]{:S(2)}, u32[]{:S(2)}) collective-permute-start(bf16[4096,128]{1,0:T(8,128)(2,1)S(1)} %copy-done.1), channel_id=1, source_target_pairs={{0,8},{8,0},{16,24},{24,16},{32,40},{40,32},{48,56},{56,48},{64,72... | collective-permute-start | bytes 3145736 | tf_op jit(solution)/shard_map/ppermute | solution.py:262
  21.9 0.1 collective-permute-start.6
  22.0 3.5 %all-to-all-start.1 = ((bf16[16,16,512]{2,1,0:T(8,128)(2,1)}), bf16[16,16,512]{2,1,0:T(8,128)(2,1)S(1)}, u32[]{:S(2)}, u32[]{:S(2)}) async-start(bf16[16,16,512]{2,1,0:T(8,128)(2,1)} %get-tuple-element.15), calls=%async_computation.1 | async-start | bytes 524288 | tf_op jit(solution)/shard_map/all_to_all | solution.py:259
  25.5 0.6 collective-permute-start.7
  26.9 0.1 collective-permute-start.4
  27.0 1.2 collective-permute-done.4.count1
  28.2 4.9 %all-to-all-done.1 = bf16[16,16,512]{2,1,0:T(8,128)(2,1)S(1)} async-done(((bf16[16,16,512]{2,1,0:T(8,128)(2,1)}), bf16[16,16,512]{2,1,0:T(8,128)(2,1)S(1)}, u32[]{:S(2)}, u32[]{:S(2)}) %all-to-all-start.1) | async-done | bytes 262176 | tf_op jit(solution)/shard_map/all_to_all | solution.py:259
  33.1 37.9 %shard_map.93 = bf16[256,640]{1,0:T(8,128)(2,1)S(1)} custom-call(s32[1]{0:T(128)S(6)} %copy.10.count0, s32[1]{0:T(128)} %collective-permute-done.4.count1, bf16[256,512]{1,0:T(8,128)(2,1)S(1)} %bitcast.8, bf16[128,128]{1,0:T(8,128)(2,1)S(1)} %slice.3.sample_keys, bf16[4096,128]{1,0:T(8,128)(2,1)S(1)} %copy-done.1, bf16[4096,128]{1,0:T(8,128)(2,1)S(1)} %copy-done.2, ...), custom_call_target="tpu_custom_call" | custom-call | tf_op jit(solution)/shard_map/pallas_call | solution.py:294
  71.0 15.8 %all_to_all.26.pieces = bf16[16,16,640]{2,1,0:T(8,128)(2,1)S(1)} all-to-all(bf16[16,16,640]{2,1,0:T(8,128)(2,1)S(1)} %bitcast.7), channel_id=1, replica_groups={{0,16,32,48,64,80,96,112,128,144,160,176,192,208,224,240},{8,24,40,56,7..., dimensions={0} | all-to-all | bytes 655360 | tf_op jit(solution)/shard_map/all_to_all | solution.py:259
  86.8 0.4 shard_map.94
  87.1 10.9 %all_to_all.27 = bf16[16,16,512]{2,1,0:T(8,128)(2,1)S(1)} all-to-all(bf16[16,16,512]{2,1,0:T(8,128)(2,1)S(1)} %shard_map.94), channel_id=1, replica_groups={{0,16,32,48,64,80,96,112,128,144,160,176,192,208,224,240},{8,24,40,56,7..., dimensions={0} | all-to-all | bytes 524288 | tf_op jit(solution)/shard_map/all_to_all | solution.py:259
  98.0 3.8 %collective-permute-start.8 = (bf16[256,512]{1,0:T(8,128)(2,1)S(1)}, bf16[256,512]{1,0:T(8,128)(2,1)S(1)}, u32[]{:S(2)}, u32[]{:S(2)}) collective-permute-start(bf16[256,512]{1,0:T(8,128)(2,1)S(1)} %bitcast.10), channel_id=1, source_target_pairs={{0,8},{8,0},{16,24},{24,16},{32,40},{40,32},{48,56},{56,48},{64,72... | collective-permute-start | bytes 786440 | tf_op jit(solution)/shard_map/ppermute | solution.py:333
  101.9 0.2 fusion.2
  102.1 0.9 collective-permute-done.8
  103.1 0.2 fusion
  103.3 15.9 %all_to_all.28.pieces = bf16[8,32,256]{2,1,0:T(8,128)(2,1)S(1)} all-to-all(bf16[8,32,256]{2,1,0:T(8,128)(2,1)S(1)} %bitcast.12), channel_id=1, replica_groups=mesh['ctx'=32,'tp'=8] {'tp'}, dimensions={0} | all-to-all | bytes 262144 | tf_op jit(solution)/shard_map/all_to_all | solution.py:342
  119.2 0.6 shard_map.95
  (15 shorter events, 0.0 us)
Async XLA Ops:
  0.0 101.9 %copy-start = (bf16[1024,256]{1,0:T(8,128)(2,1)S(1)}, bf16[1024,256]{1,0:T(8,128)(2,1)}, u32[]{:S(2)}) copy-start(bf16[1024,256]{1,0:T(8,128)(2,1)} %param.13) | copy-start | bytes 1572868
  0.0 5.4 %copy-start.3 = (bf16[256,256]{1,0:T(8,128)(2,1)S(1)}, bf16[256,256]{1,0:T(8,128)(2,1)}, u32[]{:S(2)}) copy-start(bf16[256,256]{1,0:T(8,128)(2,1)} %hidden_own.1) | copy-start | bytes 393220
  0.0 5.4 %collective-permute-start.1 = (bf16[256,1024]{1,0:T(8,128)(2,1)}, bf16[256,1024]{1,0:T(8,128)(2,1)S(1)}, u32[]{:S(2)}, u32[]{:S(2)}) collective-permute-start(bf16[256,1024]{1,0:T(8,128)(2,1)} %param.10), channel_id=1, source_target_pairs={{0,8},{8,0},{16,24},{24,16},{32,40},{40,32},{48,56},{56,48},{64,72... | collective-permute-start | bytes 1572872 | tf_op jit(solution)/shard_map/ppermute | solution.py:262
  3.2 2.1 %collective-permute-start = (bf16[256,256]{1,0:T(8,128)(2,1)}, bf16[256,256]{1,0:T(8,128)(2,1)S(1)}, u32[]{:S(2)}, u32[]{:S(2)}) collective-permute-start(bf16[256,256]{1,0:T(8,128)(2,1)} %hidden_own.1), channel_id=1, source_target_pairs={{0,8},{8,0},{16,24},{24,16},{32,40},{40,32},{48,56},{56,48},{64,72... | collective-permute-start | bytes 393224 | tf_op jit(solution)/shard_map/ppermute | solution.py:262
  3.2 2.0 %collective-permute-start.2 = (bf16[256,128]{1,0:T(8,128)(2,1)}, bf16[256,128]{1,0:T(8,128)(2,1)S(1)}, u32[]{:S(2)}, u32[]{:S(2)}) collective-permute-start(bf16[256,128]{1,0:T(8,128)(2,1)} %param.11), channel_id=1, source_target_pairs={{0,8},{8,0},{16,24},{24,16},{32,40},{40,32},{48,56},{56,48},{64,72... | collective-permute-start | bytes 196616 | tf_op jit(solution)/shard_map/ppermute | solution.py:262
  3.8 1.6 %collective-permute-start.3 = (bf16[256,128]{1,0:T(8,128)(2,1)}, bf16[256,128]{1,0:T(8,128)(2,1)S(1)}, u32[]{:S(2)}, u32[]{:S(2)}) collective-permute-start(bf16[256,128]{1,0:T(8,128)(2,1)} %param.12), channel_id=1, source_target_pairs={{0,8},{8,0},{16,24},{24,16},{32,40},{40,32},{48,56},{56,48},{64,72... | collective-permute-start | bytes 196616 | tf_op jit(solution)/shard_map/ppermute | solution.py:262
  5.9 13.8 %copy-start.1 = (bf16[4096,128]{1,0:T(8,128)(2,1)S(1)}, bf16[4096,128]{1,0:T(8,128)(2,1)}, u32[]{:S(2)}) copy-start(bf16[4096,128]{1,0:T(8,128)(2,1)} %keys0.1) | copy-start | bytes 3145732
  5.9 16.0 %copy-start.2 = (bf16[4096,128]{1,0:T(8,128)(2,1)S(1)}, bf16[4096,128]{1,0:T(8,128)(2,1)}, u32[]{:S(2)}) copy-start(bf16[4096,128]{1,0:T(8,128)(2,1)} %values0.1) | copy-start | bytes 3145732
  6.0 20.9 %copy-start.4 = (s32[256]{0:T(256)S(1)}, s32[256]{0:T(256)}, u32[]{:S(2)}) copy-start(s32[256]{0:T(256)} %param.17) | copy-start | bytes 3076
  19.7 13.3 %collective-permute-start.5 = (bf16[4096,128]{1,0:T(8,128)(2,1)S(1)}, bf16[4096,128]{1,0:T(8,128)(2,1)}, u32[]{:S(2)}, u32[]{:S(2)}) collective-permute-start(bf16[4096,128]{1,0:T(8,128)(2,1)S(1)} %copy-done.1), channel_id=1, source_target_pairs={{0,8},{8,0},{16,24},{24,16},{32,40},{40,32},{48,56},{56,48},{64,72... | collective-permute-start | bytes 3145736 | tf_op jit(solution)/shard_map/ppermute | solution.py:262
  21.9 11.2 %collective-permute-start.6 = (bf16[4096,128]{1,0:T(8,128)(2,1)S(1)}, bf16[4096,128]{1,0:T(8,128)(2,1)}, u32[]{:S(2)}, u32[]{:S(2)}) collective-permute-start(bf16[4096,128]{1,0:T(8,128)(2,1)S(1)} %copy-done.2), channel_id=1, source_target_pairs={{0,8},{8,0},{16,24},{24,16},{32,40},{40,32},{48,56},{56,48},{64,72... | collective-permute-start | bytes 3145736 | tf_op jit(solution)/shard_map/ppermute | solution.py:262
  22.0 11.1 %all-to-all-start.1 = ((bf16[16,16,512]{2,1,0:T(8,128)(2,1)}), bf16[16,16,512]{2,1,0:T(8,128)(2,1)S(1)}, u32[]{:S(2)}, u32[]{:S(2)}) async-start(bf16[16,16,512]{2,1,0:T(8,128)(2,1)} %get-tuple-element.15), calls=%async_computation.1 | async-start | bytes 524288 | tf_op jit(solution)/shard_map/all_to_all | solution.py:259
  25.5 2.6 %collective-permute-start.7 = (bf16[16,128]{1,0:T(8,128)(2,1)S(1)}, bf16[16,128]{1,0:T(8,128)(2,1)S(1)}, u32[]{:S(2)}, u32[]{:S(2)}) collective-permute-start(bf16[16,128]{1,0:T(8,128)(2,1)S(1)} %get-tuple-element.19.new_own), channel_id=1, source_target_pairs={{0,8},{8,0},{16,24},{24,16},{32,40},{40,32},{48,56},{56,48},{64,72... | collective-permute-start | bytes 12296 | tf_op jit(solution)/shard_map/ppermute | solution.py:262
  26.9 1.3 %collective-permute-start.4 = (s32[1]{0:T(128)}, s32[1]{0:T(128)}, u32[]{:S(2)}, u32[]{:S(2)}) collective-permute-start(s32[1]{0:T(128)} %param.16), channel_id=1, source_target_pairs={{0,8},{8,0},{16,24},{24,16},{32,40},{40,32},{48,56},{56,48},{64,72... | collective-permute-start | bytes 20 | tf_op jit(solution)/shard_map/ppermute | solution.py:262
  98.0 5.0 %collective-permute-start.8 = (bf16[256,512]{1,0:T(8,128)(2,1)S(1)}, bf16[256,512]{1,0:T(8,128)(2,1)S(1)}, u32[]{:S(2)}, u32[]{:S(2)}) collective-permute-start(bf16[256,512]{1,0:T(8,128)(2,1)S(1)} %bitcast.10), channel_id=1, source_target_pairs={{0,8},{8,0},{16,24},{24,16},{32,40},{40,32},{48,56},{56,48},{64,72... | collective-permute-start | bytes 786440 | tf_op jit(solution)/shard_map/ppermute | solution.py:333
